TPU v7x, 32 devices: a whole 2x2x4 slice. The times are simulated.
32 devices in a mesh: dp: 4 (over y, x), fsdp: 8 (over z, core).
Axes of the slice: x: 2, y: 2, z: 4, core: 2. Of those that a mesh axis runs over, the one named last changes fastest.
Arguments:
- tokens: bfloat16 [32, 1024, 512], P(('dp', 'fsdp')), may hold values from -6 to 6
- lengths: int32 [32], P(('dp', 'fsdp')), may hold values from 128 to 1024, as said below
- routes: int32 [32, 1024, 8], P(('dp', 'fsdp')), may hold values from 0 to 23, all different within a row
- query_weight: bfloat16 [512, 1536], P(('dp', 'fsdp')), may hold values from -0.25 to 0.25
- key_value_weight: bfloat16 [512, 128], P(('dp', 'fsdp')), may hold values from -0.25 to 0.25
- router_weight: bfloat16 [512, 24], P(('dp', 'fsdp')), may hold values from -0.125 to 0.125
- output_weight: bfloat16 [1536, 512], P(('dp', 'fsdp')), may hold values from -16 to 16
- expand_weight: bfloat16 [512, 2048], P(('dp', 'fsdp')), may hold values from -0.25 to 0.25
- expand_bias: bfloat16 [2048], P(('dp', 'fsdp')), may hold values from -3 to 3
- reduce_weight: bfloat16 [2048, 512], P(('dp', 'fsdp')), may hold values from -0.1875 to 0.1875
- reduce_bias: bfloat16 [512], P(('dp', 'fsdp')), may hold values from -1.75 to 1.75
- first_gain: bfloat16 [512], P(('dp', 'fsdp')), may hold values from 0.25 to 1.75
- first_bias: bfloat16 [512], P(('dp', 'fsdp')), may hold values from -1.75 to 1.75
- second_gain: bfloat16 [512], P(('dp', 'fsdp')), may hold values from 0.25 to 1.75
- second_bias: bfloat16 [512], P(('dp', 'fsdp')), may hold values from -1.75 to 1.75
- cotangent: bfloat16 [32, 1024, 512], P(('dp', 'fsdp')), may hold values from -6 to 6
Outputs:
- output: bfloat16 [32, 1024, 512], P(('dp', 'fsdp'))
- tokens_grad: bfloat16 [32, 1024, 512], P(('dp', 'fsdp'))
- query_weight_grad: float32 [512, 1536], P(('dp', 'fsdp'))
- key_value_weight_grad: float32 [512, 128], P(('dp', 'fsdp'))
- router_weight_grad: float32 [512, 24], P(('dp', 'fsdp'))
- output_weight_grad: float32 [1536, 512], P(('dp', 'fsdp'))
- expand_weight_grad: float32 [512, 2048], P(('dp', 'fsdp'))
- expand_bias_grad: float32 [2048], P(('dp', 'fsdp'))
- reduce_weight_grad: float32 [2048, 512], P(('dp', 'fsdp'))
- reduce_bias_grad: float32 [512], P(('dp', 'fsdp'))
- first_gain_grad: float32 [512], P(('dp', 'fsdp'))
- first_bias_grad: float32 [512], P(('dp', 'fsdp'))
- second_gain_grad: float32 [512], P(('dp', 'fsdp'))
- second_bias_grad: float32 [512], P(('dp', 'fsdp'))
- router_stats: float32 [2, 24], replicated
Inputs may be any that keep to these rules, and one draw needn't show every extreme that they name: Sequence s holds valid tokens at slots below lengths[s], padding after them; some sequence has exactly 1024. `routes`: each token names 8 different head experts.
All inputs are finite; a program needn't handle non-finite values.
Results may differ from a plain program's by a relative error of at most 0.012.
Values may be sent and summed in bfloat16 or wider, within the bound.
No kernel may reach another device: no remote copies, remote signals or barrier semaphores. Data moves between devices by JAX's collectives and lax.ppermute only.
A program may use at most 128 MiB of HBM per device.

v0:
```python
import jax
import jax.numpy as jnp
from jax import lax
from jax.sharding import PartitionSpec as P

D = 512
HD = 64
E = 24
TOPK = 8
LEN = 1024
QB = 512


def layer_norm(values, norm_gain, norm_bias):
    center = values - jnp.mean(values, axis=-1, keepdims=True)
    spread = jnp.mean(center * center, axis=-1, keepdims=True)
    return center * lax.rsqrt(spread + 1e-05) * norm_gain + norm_bias


def masked_scores(query_block, key_rows, start, length):
    scores = jnp.einsum(
        "tjd,sd->tjs", query_block, key_rows, preferred_element_type=jnp.float32
    ) * HD ** (-0.5)
    places = jnp.arange(LEN)
    at_rows = start + jnp.arange(QB)
    allowed = (places[None, :] <= at_rows[:, None]) & (places[None, :] < length)
    return jnp.where(allowed[:, None, :], scores, -1e30)


def attend_forward(seq_item):
    query_seq, key_rows, value_rows, length = seq_item

    def one_block(block_item):
        query_block, start = block_item
        scores = masked_scores(query_block, key_rows, start, length)
        summit = jnp.max(scores, axis=-1, keepdims=True)
        expo_part = jnp.exp(scores - summit)
        totals = jnp.sum(expo_part, axis=-1, keepdims=True)
        soft_low = (expo_part / totals).astype(jnp.bfloat16)
        mixed_out = jnp.einsum(
            "tjs,sd->tjd", soft_low, value_rows, preferred_element_type=jnp.float32
        )
        return (mixed_out, summit[..., 0] + jnp.log(totals[..., 0]))

    starts = jnp.arange(query_seq.shape[0]) * QB
    return lax.map(one_block, (query_seq, starts))


def attend_backward(seq_item):
    query_seq, key_rows, value_rows, grad_seq, total_seq, length = seq_item

    def one_block(running, block_item):
        key_sum, value_sum = running
        query_block, grad_block, total_block, start = block_item
        scores = masked_scores(query_block, key_rows, start, length)
        soft_full = jnp.exp(scores - total_block[..., None])
        soft_low = soft_full.astype(jnp.bfloat16)
        value_sum = value_sum + jnp.einsum(
            "tjs,tjd->sd", soft_low, grad_block, preferred_element_type=jnp.float32
        )
        prob_grad = jnp.einsum(
            "tjd,sd->tjs", grad_block, value_rows, preferred_element_type=jnp.float32
        )
        score_grad = (
            soft_full * (prob_grad - jnp.sum(soft_full * prob_grad, axis=-1, keepdims=True))
        ).astype(jnp.bfloat16)
        query_grad = jnp.einsum(
            "tjs,sd->tjd", score_grad, key_rows, preferred_element_type=jnp.float32
        ) * HD ** (-0.5)
        key_sum = key_sum + jnp.einsum(
            "tjs,tjd->sd", score_grad, query_block, preferred_element_type=jnp.float32
        ) * HD ** (-0.5)
        return ((key_sum, value_sum), query_grad)

    zero_block = jnp.zeros((LEN, HD), jnp.float32)
    starts = jnp.arange(query_seq.shape[0]) * QB
    (key_grad, value_grad), query_grad = lax.scan(
        one_block, (zero_block, zero_block), (query_seq, grad_seq, total_seq, starts)
    )
    return (query_grad, key_grad, value_grad)


def per_device(
    tokens,
    lengths,
    routes,
    query_weight,
    key_value_weight,
    router_weight,
    output_weight,
    expand_weight,
    expand_bias,
    reduce_weight,
    reduce_bias,
    first_gain,
    first_bias,
    second_gain,
    second_bias,
    cotangent,
):
    gathered = (
        lax.all_gather(query_weight, ("dp", "fsdp"), axis=0, tiled=True),
        lax.all_gather(key_value_weight, ("dp", "fsdp"), axis=0, tiled=True),
        lax.all_gather(router_weight, ("dp", "fsdp"), axis=0, tiled=True),
        lax.all_gather(output_weight, ("dp", "fsdp"), axis=0, tiled=True),
        lax.all_gather(expand_weight, ("dp", "fsdp"), axis=0, tiled=True),
        lax.all_gather(expand_bias, ("dp", "fsdp"), axis=0, tiled=True),
        lax.all_gather(reduce_weight, ("dp", "fsdp"), axis=0, tiled=True),
        lax.all_gather(reduce_bias, ("dp", "fsdp"), axis=0, tiled=True),
        lax.all_gather(first_gain, ("dp", "fsdp"), axis=0, tiled=True),
        lax.all_gather(first_bias, ("dp", "fsdp"), axis=0, tiled=True),
        lax.all_gather(second_gain, ("dp", "fsdp"), axis=0, tiled=True),
        lax.all_gather(second_bias, ("dp", "fsdp"), axis=0, tiled=True),
    )
    (
        full_query,
        full_key_value,
        full_router,
        full_output,
        full_expand,
        full_expand_bias,
        full_reduce,
        full_reduce_bias,
        gain_one,
        bias_one,
        gain_two,
        bias_two,
    ) = gathered
    seq_count = tokens.shape[0]
    row_count = seq_count * LEN
    blocks = LEN // QB
    inputs = tokens.reshape(row_count, D).astype(jnp.float32)
    route_flat = routes.reshape(row_count, TOPK)
    onehot = (route_flat[:, :, None] == jnp.arange(E)[None, None, :]).astype(jnp.float32)
    onehot_low = onehot.astype(jnp.bfloat16)
    valid_rows = (
        (jnp.arange(LEN)[None, :] < lengths[:, None]).astype(jnp.float32).reshape(row_count)
    )
    normed_full, first_pull = jax.vjp(
        layer_norm, inputs, gain_one.astype(jnp.float32), bias_one.astype(jnp.float32)
    )
    normed = normed_full.astype(jnp.bfloat16)
    query_all = jnp.dot(normed, full_query, preferred_element_type=jnp.float32).reshape(
        row_count, E, HD
    )
    queries = jnp.take_along_axis(query_all, route_flat[:, :, None], axis=1).astype(jnp.bfloat16)
    key_value = jnp.dot(normed, full_key_value, preferred_element_type=jnp.float32).astype(
        jnp.bfloat16
    )
    logits = jnp.dot(normed, full_router, preferred_element_type=jnp.float32)
    router_probs = jax.nn.softmax(logits, axis=-1)

    def gate_of(logit_values):
        picked = jnp.take_along_axis(logit_values, route_flat, axis=1)
        return jax.nn.softmax(picked, axis=-1)

    gating, gate_pull = jax.vjp(gate_of, logits)
    query_seq = queries.reshape(seq_count, blocks, QB, TOPK, HD)
    key_seq = key_value[:, :HD].reshape(seq_count, LEN, HD)
    value_seq = key_value[:, HD:].reshape(seq_count, LEN, HD)
    mixed_out, log_total = lax.map(attend_forward, (query_seq, key_seq, value_seq, lengths))
    mixed_out = mixed_out.reshape(row_count, TOPK, HD)
    spread_out = (
        jnp.einsum(
            "tje,tjd->ted", onehot, gating[:, :, None] * mixed_out, precision=lax.Precision.HIGHEST
        )
        .reshape(row_count, E * HD)
        .astype(jnp.bfloat16)
    )
    attended = jnp.dot(spread_out, full_output, preferred_element_type=jnp.float32)
    middle = inputs + attended
    normed_two_full, second_pull = jax.vjp(
        layer_norm, middle, gain_two.astype(jnp.float32), bias_two.astype(jnp.float32)
    )
    normed_two = normed_two_full.astype(jnp.bfloat16)
    expanded = jnp.dot(
        normed_two, full_expand, preferred_element_type=jnp.float32
    ) + full_expand_bias.astype(jnp.float32)
    activated_full, gelu_pull = jax.vjp(jax.nn.gelu, expanded)
    activated = activated_full.astype(jnp.bfloat16)
    reduced = jnp.dot(
        activated, full_reduce, preferred_element_type=jnp.float32
    ) + full_reduce_bias.astype(jnp.float32)
    output = (middle + reduced).astype(jnp.bfloat16).reshape(tokens.shape)
    counts = jnp.sum(valid_rows[:, None, None] * onehot, axis=(0, 1))
    prob_sums = jnp.sum(router_probs * valid_rows[:, None], axis=0)
    counts_all, prob_all = lax.psum((counts, prob_sums), ("dp", "fsdp"))
    valid_total = jnp.sum(counts_all) / TOPK
    router_stats = jnp.stack([E * counts_all / (TOPK * valid_total), E * prob_all / valid_total])
    regathered = (
        lax.all_gather(query_weight, ("dp", "fsdp"), axis=0, tiled=True),
        lax.all_gather(key_value_weight, ("dp", "fsdp"), axis=0, tiled=True),
        lax.all_gather(router_weight, ("dp", "fsdp"), axis=0, tiled=True),
        lax.all_gather(output_weight, ("dp", "fsdp"), axis=0, tiled=True),
        lax.all_gather(expand_weight, ("dp", "fsdp"), axis=0, tiled=True),
        lax.all_gather(reduce_weight, ("dp", "fsdp"), axis=0, tiled=True),
    )
    back_query, back_key_value, back_router, back_output, back_expand, back_reduce = regathered
    grad_out = cotangent.reshape(row_count, D)
    grad_full = grad_out.astype(jnp.float32)
    reduce_weight_grad = jnp.einsum(
        "tf,td->fd", activated, grad_out, preferred_element_type=jnp.float32
    )
    reduce_bias_grad = jnp.sum(grad_full, axis=0)
    (expanded_grad,) = gelu_pull(
        jnp.einsum("td,fd->tf", grad_out, back_reduce, preferred_element_type=jnp.float32)
    )
    expanded_low = expanded_grad.astype(jnp.bfloat16)
    expand_weight_grad = jnp.einsum(
        "td,tf->df", normed_two, expanded_low, preferred_element_type=jnp.float32
    )
    expand_bias_grad = jnp.sum(expanded_low.astype(jnp.float32), axis=0)
    middle_part, second_gain_grad, second_bias_grad = second_pull(
        jnp.einsum("tf,df->td", expanded_low, back_expand, preferred_element_type=jnp.float32)
    )
    middle_grad = grad_full + middle_part
    attended_low = middle_grad.astype(jnp.bfloat16)
    output_weight_grad = jnp.einsum(
        "te,td->ed", spread_out, attended_low, preferred_element_type=jnp.float32
    )
    spread_grad = jnp.einsum(
        "td,ed->te", attended_low, back_output, preferred_element_type=jnp.float32
    ).reshape(row_count, E, HD)
    slot_grad = jnp.take_along_axis(spread_grad, route_flat[:, :, None], axis=1)
    mixed_low = (gating[:, :, None] * slot_grad).astype(jnp.bfloat16)
    (logit_grad,) = gate_pull(jnp.sum(mixed_out * slot_grad, axis=-1))
    logit_low = logit_grad.astype(jnp.bfloat16)
    router_weight_grad = jnp.einsum(
        "td,te->de", normed, logit_low, preferred_element_type=jnp.float32
    )
    query_grad, key_grad, value_grad = lax.map(
        attend_backward,
        (
            query_seq,
            key_seq,
            value_seq,
            mixed_low.reshape(seq_count, blocks, QB, TOPK, HD),
            log_total,
            lengths,
        ),
    )
    key_value_grad = (
        jnp.concatenate([key_grad, value_grad], axis=-1)
        .reshape(row_count, 2 * HD)
        .astype(jnp.bfloat16)
    )
    query_low = query_grad.reshape(row_count, TOPK, HD).astype(jnp.bfloat16)
    query_all_grad = (
        jnp.einsum("tje,tjd->ted", onehot_low, query_low, preferred_element_type=jnp.float32)
        .reshape(row_count, E * HD)
        .astype(jnp.bfloat16)
    )
    query_weight_grad = jnp.einsum(
        "td,te->de", normed, query_all_grad, preferred_element_type=jnp.float32
    )
    key_value_weight_grad = jnp.einsum(
        "td,te->de", normed, key_value_grad, preferred_element_type=jnp.float32
    )
    normed_grad = (
        jnp.einsum("te,de->td", query_all_grad, back_query, preferred_element_type=jnp.float32)
        + jnp.einsum(
            "te,de->td", key_value_grad, back_key_value, preferred_element_type=jnp.float32
        )
        + jnp.einsum("te,de->td", logit_low, back_router, preferred_element_type=jnp.float32)
    )
    input_part, first_gain_grad, first_bias_grad = first_pull(normed_grad)
    tokens_grad = (middle_grad + input_part).astype(jnp.bfloat16).reshape(tokens.shape)
    grad_shards = (
        lax.psum_scatter(query_weight_grad, ("dp", "fsdp"), scatter_dimension=0, tiled=True),
        lax.psum_scatter(key_value_weight_grad, ("dp", "fsdp"), scatter_dimension=0, tiled=True),
        lax.psum_scatter(router_weight_grad, ("dp", "fsdp"), scatter_dimension=0, tiled=True),
        lax.psum_scatter(output_weight_grad, ("dp", "fsdp"), scatter_dimension=0, tiled=True),
        lax.psum_scatter(expand_weight_grad, ("dp", "fsdp"), scatter_dimension=0, tiled=True),
        lax.psum_scatter(expand_bias_grad, ("dp", "fsdp"), scatter_dimension=0, tiled=True),
        lax.psum_scatter(reduce_weight_grad, ("dp", "fsdp"), scatter_dimension=0, tiled=True),
        lax.psum_scatter(reduce_bias_grad, ("dp", "fsdp"), scatter_dimension=0, tiled=True),
        lax.psum_scatter(first_gain_grad, ("dp", "fsdp"), scatter_dimension=0, tiled=True),
        lax.psum_scatter(first_bias_grad, ("dp", "fsdp"), scatter_dimension=0, tiled=True),
        lax.psum_scatter(second_gain_grad, ("dp", "fsdp"), scatter_dimension=0, tiled=True),
        lax.psum_scatter(second_bias_grad, ("dp", "fsdp"), scatter_dimension=0, tiled=True),
    )
    return (output, tokens_grad) + tuple(grad_shards) + (router_stats,)


def solution(mesh):
    in_specs = (
        P(("dp", "fsdp"), None, None),
        P(("dp", "fsdp")),
        P(("dp", "fsdp"), None, None),
        P(("dp", "fsdp"), None),
        P(("dp", "fsdp"), None),
        P(("dp", "fsdp"), None),
        P(("dp", "fsdp"), None),
        P(("dp", "fsdp"), None),
        P(("dp", "fsdp")),
        P(("dp", "fsdp"), None),
        P(("dp", "fsdp")),
        P(("dp", "fsdp")),
        P(("dp", "fsdp")),
        P(("dp", "fsdp")),
        P(("dp", "fsdp")),
        P(("dp", "fsdp"), None, None),
    )
    out_specs = (
        P(("dp", "fsdp"), None, None),
        P(("dp", "fsdp"), None, None),
        P(("dp", "fsdp"), None),
        P(("dp", "fsdp"), None),
        P(("dp", "fsdp"), None),
        P(("dp", "fsdp"), None),
        P(("dp", "fsdp"), None),
        P(("dp", "fsdp")),
        P(("dp", "fsdp"), None),
        P(("dp", "fsdp")),
        P(("dp", "fsdp")),
        P(("dp", "fsdp")),
        P(("dp", "fsdp")),
        P(("dp", "fsdp")),
        P(),
    )
    return jax.shard_map(
        per_device, mesh=mesh, in_specs=in_specs, out_specs=out_specs, check_vma=False
    )
```

profile of v0, /device:TPU:0, one launch (start us, length us, event | category | flops | bytes accessed | tf_op | source)
XLA Modules:
  0.0 1515.1 jit_solution(15340609358197634253)
XLA Ops:
  18.4 42.3 %all-reduce.13 = (bf16[512]{0:T(512)(128)(2,1)S(1)}, bf16[512]{0:T(512)(128)(2,1)S(1)}, bf16[512]{0:T(512)(128)(2,1)}, bf16[512]{0:T(512)(128)(2,1)}, bf16[512]{0:T(512)(128)(2,1)}, /*index=5*/bf16[2048]{0:T(1024)(128)(2,1)}) all-reduce(bf16[512]{0:T(512)(128)(2,1)S(1)} %dynamic-update-slice.1, ...), channel_id=1, replica_groups=mesh['dp'=4,'fsdp'=8] {'dp','fsdp'}, use_global_device_ids=true, to_apply=%add.1 | all-reduce | flops 4608 | bytes 18432
  60.7 41.2 %all_gather.44 = bf16[512,24]{1,0:T(8,128)(2,1)S(1)} all-gather(bf16[16,24]{1,0:T(8,128)(2,1)} %param.27), channel_id=1, replica_groups=mesh['dp'=4,'fsdp'=8] {'dp','fsdp'}, dimensions={0}, use_global_device_ids=true | all-gather | bytes 25344 | tf_op jit(solution)/shard_map/all_gather | solution.py:104
  107.5 65.5 %gather_fusion = f32[8192]{0:T(1024)S(1)} fusion(f32[1024,24]{0,1:T(8,128)S(1)} %get-tuple-element.375, s32[8192]{0:T(1024)S(1)} %reshape.462), kind=kCustom, calls=%fused_computation.2 | custom fusion | bytes 131072 | tf_op jit(solution)/shard_map/jvp(jit(take_along_axis))/gather | solution.py:154
  176.8 37.2 %all_gather.46 = bf16[512,128]{1,0:T(8,128)(2,1)S(1)} all-gather(bf16[16,128]{1,0:T(8,128)(2,1)S(1)} %copy-done.83), channel_id=1, replica_groups=mesh['dp'=4,'fsdp'=8] {'dp','fsdp'}, dimensions={0}, use_global_device_ids=true | all-gather | bytes 135168 | tf_op jit(solution)/shard_map/all_gather | solution.py:103
  231.8 98.5 %gather_fusion.1 = bf16[8192,64]{1,0:T(8,128)(2,1)S(1)} fusion(bf16[1024,24,64]{2,1,0:T(8,128)(2,1)} %copy.86, s32[8192]{0:T(1024)S(1)} %reshape.462), kind=kCustom, calls=%fused_computation.clone | custom fusion | bytes 2162688 | tf_op jit(solution)/shard_map/jit(take_along_axis)/gather | solution.py:146
  332.1 73.9 %while.47 = (s32[]{:T(128)}, f32[2,512,8,64]{1,0,3,2:T(2,128)}, f32[2,512,8]{1,2,0:T(8,128)}, s32[2]{0:T(128)S(1)}, s32[]{:T(128)}, /*index=5*/bf16[2,512,8,64]{...) while((s32[]{:T(128)}, f32[2,512,8,64]{1,0,3,2:T(2,128)}, ...), condition=%wide.region_7.9_spmd, body=%wide.region_4.8_spmd.sunk | while | flops 1125119488 | bytes 58595468 | solution.py:46
  349.6 19.5 %dynamic_update_slice.31 = f32[2,512,8,64]{1,0,3,2:T(2,128)} dynamic-update-slice(f32[2,512,8,64]{1,0,3,2:T(2,128)} %get-tuple-element.513, f32[1,512,8,64]{1,0,3,2:T(1,128)S(1)} %copy.151, s32[]{:T(128)S(6)} %copy.164, s32[]{:T(128)} %constant.110.clone.1..sunk, s32[]{:T(128)} %constant.110.clone.1..sunk, s32[]{:T(128)} %constant.110.clone.1..sunk) | dynamic-update-slice | bytes 2097156 | tf_op jit(solution)/shard_map/while/body/eval_jaxpr/while/body/jit(dynamic_update_index_in_dim)/dynamic_update_slice | solution.py:46
  386.5 19.5 %dynamic_update_slice.31 = f32[2,512,8,64]{1,0,3,2:T(2,128)} dynamic-update-slice(f32[2,512,8,64]{1,0,3,2:T(2,128)} %get-tuple-element.513, f32[1,512,8,64]{1,0,3,2:T(1,128)S(1)} %copy.151, s32[]{:T(128)S(6)} %copy.164, s32[]{:T(128)} %constant.110.clone.1..sunk, s32[]{:T(128)} %constant.110.clone.1..sunk, s32[]{:T(128)} %constant.110.clone.1..sunk) | dynamic-update-slice | bytes 2097156 | tf_op jit(solution)/shard_map/while/body/eval_jaxpr/while/body/jit(dynamic_update_index_in_dim)/dynamic_update_slice | solution.py:46
  417.4 15.7 %fusion.50 = bf16[1024,24,64]{2,1,0:T(8,128)(2,1)} fusion(f32[1024,8,64]{2,1,0:T(8,128)} %copy.90, s32[1024,8]{1,0:T(8,128)S(1)} %copy-done.24), kind=kOutput, calls=%fused_computation.73 | convolution fusion | flops 152764416 | bytes 5275648 | tf_op jit(solution)/shard_map/tje,tjd->ted/dot_general | solution.py:164
  454.9 11.1 convert_reduce_fusion
  484.2 9.7 copy.97
  493.8 118.6 %gather_fusion.2 = f32[8192,64]{1,0:T(8,128)} fusion(f32[1024,24,64]{2,1,0:T(8,128)} %copy.97, s32[8192]{0:T(1024)S(1)} %copy-done.3), kind=kCustom, calls=%fused_computation.1.clone | custom fusion | bytes 4259840 | tf_op jit(solution)/shard_map/jit(take_along_axis)/gather | solution.py:224
  621.0 76.4 %while.48 = (s32[]{:T(128)}, f32[1024,64]{0,1:T(8,128)}, f32[1024,64]{0,1:T(8,128)}, bf16[2,512,8,64]{1,3,2,0:T(8,128)(2,1)}, s32[2]{0:T(128)S(1)}, /*index=5*/s...) while((s32[]{:T(128)}, f32[1024,64]{0,1:T(8,128)}, ...), condition=%wide.region_14.16_spmd.clone, body=%wide.region_12.15_spmd.clone.sunk | while | flops 2723739136 | bytes 149379536 | solution.py:77
  629.1 10.4 multiply_reduce_fusion.9
  667.2 10.4 multiply_reduce_fusion.9
  700.7 43.5 %scatter_custom_fusion = f32[24576]{0:T(1024)S(1)} fusion(s32[8192]{0:T(1024)} %reshape.468, f32[8192]{0:T(1024)S(1)} %reshape.470, f32[]{:T(128)} %constant.132.clone.1), kind=kCustom, calls=%fused_computation.143 | custom fusion | flops 8192 | bytes 98816
  780.5 9.6 fusion.73
  805.5 8.8 fusion.70
  825.0 39.4 %all-reduce.12 = (f32[2048]{0:T(1024)S(1)}, f32[512]{0:T(512)S(1)}, f32[512]{0:T(512)S(1)}, f32[512]{0:T(512)S(1)}, f32[512]{0:T(512)S(1)}, /*index=5*/f32[512]{0:T(512)S(1)}, f32[24]{0:T(128)S(1)}, f32[24]{0:T(128)S(1)}) all-reduce(f32[2048]{0:T(1024)S(1)} %copy-done.79, ...), channel_id=7, replica_groups=mesh['dp'=4,'fsdp'=8] {'dp','fsdp'}, use_global_device_ids=true, to_apply=%region_26.28.clone | all-reduce | flops 4656 | bytes 37248
  878.2 132.5 %reduce-scatter.9.cloned.1.call-done = f32[16,128]{1,0:T(8,128)} async-done(((f32[512,128]{1,0:T(8,128)}), f32[16,128]{1,0:T(8,128)}) %reduce-scatter.9.cloned.1.call-update) | async-done | bytes 8208 | tf_op jit(solution)/shard_map/reduce_scatter | solution.py:270
  1010.7 103.8 %reduce-scatter.13.cloned.1.call-done = f32[48,512]{1,0:T(8,128)} async-done(((f32[1536,512]{1,0:T(8,128)}), f32[48,512]{1,0:T(8,128)}) %reduce-scatter.13.cloned.1.call-update) | async-done | bytes 98320 | tf_op jit(solution)/shard_map/reduce_scatter | solution.py:272
  1114.5 106.5 %reduce-scatter.7.cloned.1.call-done = f32[16,1536]{1,0:T(8,128)} async-done(((f32[512,1536]{1,0:T(8,128)}), f32[16,1536]{1,0:T(8,128)}) %reduce-scatter.7.cloned.1.call-update) | async-done | bytes 98320 | tf_op jit(solution)/shard_map/reduce_scatter | solution.py:269
  1221.0 144.4 %reduce-scatter.17.cloned.1.call-done = f32[64,512]{1,0:T(8,128)} async-done(((f32[2048,512]{1,0:T(8,128)}), f32[64,512]{1,0:T(8,128)}) %reduce-scatter.17.cloned.1.call-update) | async-done | bytes 131088 | tf_op jit(solution)/shard_map/reduce_scatter | solution.py:275
  1365.4 142.4 %reduce-scatter.15.cloned.1.call-done = f32[16,2048]{1,0:T(8,128)} async-done(((f32[512,2048]{1,0:T(8,128)}), f32[16,2048]{1,0:T(8,128)}) %reduce-scatter.15.cloned.1.call-update) | async-done | bytes 131088 | tf_op jit(solution)/shard_map/reduce_scatter | solution.py:273
  (395 shorter events, 266.6 us)
Async XLA Ops:
  7.2 211.3 %all-gather.5.cloned.1.call-start = ((), (), s32[]{:S(2)}) async-start(), calls=%async_computation.6 | async-start | bytes 1622016 | tf_op jit(solution)/shard_map/all_gather | solution.py:102
  7.9 432.9 %all-gather.7.cloned.1.call-start = ((), (), s32[]{:S(2)}) async-start(), calls=%async_computation.7 | async-start | bytes 1622016 | tf_op jit(solution)/shard_map/all_gather | solution.py:105
  8.7 438.0 %all-gather.9.cloned.1.call-start = ((), (), s32[]{:S(2)}) async-start(), calls=%async_computation.8 | async-start | bytes 2162688 | tf_op jit(solution)/shard_map/all_gather | solution.py:106
  9.4 445.5 %all-gather.11.cloned.1.call-start = ((), (), s32[]{:S(2)}) async-start(), calls=%async_computation.9 | async-start | bytes 2162688 | tf_op jit(solution)/shard_map/all_gather | solution.py:108
  10.0 868.2 %reduce-scatter.11.cloned.1.call-start = ((), (), s32[]{:S(2)}) async-start(), calls=%async_computation.12 | async-start | bytes 270336 | tf_op jit(solution)/shard_map/reduce_scatter | solution.py:271
  102.4 129.3 %copy-start.2 = (s32[8192]{0:T(1024)}, s32[8192]{0:T(1024)S(1)}, u32[]{:S(2)}) copy-start(s32[8192]{0:T(1024)S(1)} %reshape.462) | copy-start | bytes 98308
  107.4 65.6 %copy-start = (f32[1024,24]{0,1:T(8,128)}, f32[1024,24]{0,1:T(8,128)S(1)}, u32[]{:S(2)}) copy-start(f32[1024,24]{0,1:T(8,128)S(1)} %get-tuple-element.375) | copy-start | bytes 294916
  107.4 66.1 %copy-start.43 = (s32[1,1024,8]{1,2,0:T(8,128)S(1)}, s32[1,1024,8]{1,2,0:T(8,128)}, u32[]{:S(2)}) copy-start(s32[1,1024,8]{1,2,0:T(8,128)} %param.24) | copy-start | bytes 98308
  107.4 67.5 %copy-start.91 = (bf16[512]{0:T(512)(128)(2,1)S(1)}, bf16[512]{0:T(512)(128)(2,1)}, u32[]{:S(2)}) copy-start(bf16[512]{0:T(512)(128)(2,1)} %get-tuple-element.349) | copy-start | bytes 3076
  107.4 68.0 %copy-start.90 = (bf16[512]{0:T(512)(128)(2,1)S(1)}, bf16[512]{0:T(512)(128)(2,1)}, u32[]{:S(2)}) copy-start(bf16[512]{0:T(512)(128)(2,1)} %get-tuple-element.348) | copy-start | bytes 3076
  107.4 68.6 %copy-start.84 = (bf16[2048]{0:T(1024)(128)(2,1)S(1)}, bf16[2048]{0:T(1024)(128)(2,1)}, u32[]{:S(2)}) copy-start(bf16[2048]{0:T(1024)(128)(2,1)} %get-tuple-element.350) | copy-start | bytes 12292
  107.4 69.2 %copy-start.44 = (s32[1024,8,1]{0,1,2:T(8,128)S(1)}, s32[1024,8,1]{0,1,2:T(8,128)}, u32[]{:S(2)}) copy-start(s32[1024,8,1]{0,1,2:T(8,128)} %get-tuple-element.365) | copy-start | bytes 98308
  107.4 69.2 %copy-start.93 = (s32[2]{0:T(128)S(1)}, s32[2]{0:T(128)}, u32[]{:S(2)}) copy-start(s32[2]{0:T(128)} %constant.164) | copy-start | bytes 28
  107.5 69.3 %copy-start.92 = (s32[2]{0:T(128)S(1)}, s32[2]{0:T(128)}, u32[]{:S(2)}) copy-start(s32[2]{0:T(128)} %constant.161) | copy-start | bytes 28
  107.5 69.4 %copy-start.83 = (bf16[16,128]{1,0:T(8,128)(2,1)S(1)}, bf16[16,128]{1,0:T(8,128)(2,1)}, u32[]{:S(2)}) copy-start(bf16[16,128]{1,0:T(8,128)(2,1)} %param.26) | copy-start | bytes 12292
  697.5 49.3 %copy-start.48 = (f32[1024]{0:T(1024)S(1)}, f32[1024]{0:T(1024)}, u32[]{:S(2)}) copy-start(f32[1024]{0:T(1024)} %copy-done.46) | copy-start | bytes 12292
  697.5 49.3 %copy-start.56 = (f32[1024]{0:T(1024)S(1)}, f32[1024]{0:T(1024)}, u32[]{:S(2)}) copy-start(f32[1024]{0:T(1024)} %copy-done.54) | copy-start | bytes 12292
  697.5 49.3 %copy-start.64 = (f32[512]{0:T(512)S(1)}, f32[512]{0:T(512)}, u32[]{:S(2)}) copy-start(f32[512]{0:T(512)} %copy-done.62) | copy-start | bytes 6148
  697.5 49.3 %copy-start.82 = (f32[512]{0:T(512)S(1)}, f32[512]{0:T(512)}, u32[]{:S(2)}) copy-start(f32[512]{0:T(512)} %copy-done.80) | copy-start | bytes 6148
  746.7 264.0 %reduce-scatter.9.cloned.1.call-start = ((), (), s32[]{:S(2)}) async-start(), calls=%async_computation.11 | async-start | bytes 270336 | tf_op jit(solution)/shard_map/reduce_scatter | solution.py:270
  748.1 366.4 %reduce-scatter.13.cloned.1.call-start = ((), (), s32[]{:S(2)}) async-start(), calls=%async_computation.13 | async-start | bytes 3244032 | tf_op jit(solution)/shard_map/reduce_scatter | solution.py:272
  753.7 467.2 %reduce-scatter.7.cloned.1.call-start = ((), (), s32[]{:S(2)}) async-start(), calls=%async_computation.10 | async-start | bytes 3244032 | tf_op jit(solution)/shard_map/reduce_scatter | solution.py:269
  779.3 586.1 %reduce-scatter.17.cloned.1.call-start = ((), (), s32[]{:S(2)}) async-start(), calls=%async_computation.15 | async-start | bytes 4325376 | tf_op jit(solution)/shard_map/reduce_scatter | solution.py:275
  790.2 717.6 %reduce-scatter.15.cloned.1.call-start = ((), (), s32[]{:S(2)}) async-start(), calls=%async_computation.14 | async-start | bytes 4325376 | tf_op jit(solution)/shard_map/reduce_scatter | solution.py:273
  (93 other events, 662.7 us)
Sparse Core Ops, SparseCore 0:
  11.0 58.1 all-gather.4
  72.2 53.9 all-gather.6
  129.2 55.3 all-gather.8
  187.5 55.3 all-gather.10
  746.8 131.3 reduce-scatter.10
  881.0 129.6 reduce-scatter.8
  1016.7 97.7 reduce-scatter.12
  1120.5 100.4 reduce-scatter.6
  1223.8 141.5 reduce-scatter.16
  1368.1 139.6 reduce-scatter.14
where the time goes:
time: 1530 us; the launch traced here: 1520 us
  waiting for transfers between devices  639 us (42%)
  local copies, waits for them, and re-layouts  415 us (27%)
  matrix products  174 us (11%)
  blocking collectives  160 us (10%)
  other arithmetic  108 us (7%)
  between operations  17.1 us (1%)
    reduce_scatter x1, waiting for transfers between devices, per_device(): lax.psum_scatter(reduce_weight_grad, ('dp', 'fsdp'), scatter_dimension=0,...  144 us
    reduce_scatter x1, waiting for transfers between devices, per_device(): lax.psum_scatter(expand_weight_grad, ('dp', 'fsdp'), scatter_dimension=0,...  142 us
    reduce_scatter x1, waiting for transfers between devices, per_device(): lax.psum_scatter(key_value_weight_grad, ('dp', 'fsdp'), scatter_dimension...  132 us
    gather x2, local copies, waits for them, and re-layouts, per_device(): slot_grad = jnp.take_along_axis(spread_grad, route_flat[:, :, None], axis=1)  122 us
    reduce_scatter x1, waiting for transfers between devices, per_device(): lax.psum_scatter(query_weight_grad, ('dp', 'fsdp'), scatter_dimension=0,...  106 us
    reduce_scatter x1, waiting for transfers between devices, per_device(): lax.psum_scatter(output_weight_grad, ('dp', 'fsdp'), scatter_dimension=0,...  104 us
    gather x2, local copies, waits for them, and re-layouts, per_device(): jnp.take_along_axis(query_all, route_flat[:, :, None], axis=1)  99.9 us
    unnamed x2, blocking collectives  81.7 us
  transfers between devices with their start and end apart: 10, of which 6 were waited for; matrix products, arithmetic and copies ran while one was open for 26% of the time, Pallas kernels for 0%

commit v1 on v0

v1 whole, which is shorter than its diff:
```python
import functools
import math

import jax
import jax.numpy as jnp
from jax import lax
from jax.experimental import pallas as pl
from jax.experimental.pallas import tpu as pltpu
from jax.sharding import PartitionSpec as P

D = 512
HD = 64
E = 24
TOPK = 8
FF = 2048
T = 1024
NB = 32
QW = E * HD
C1 = QW + 256
MISC = QW + 128
C2 = 3 * 512 + FF + 4 * 512
VG = E
ST = 40
SCALE2 = HD**-0.5 * math.log2(math.e)
NEG = -1e30
BF = jnp.bfloat16
F32 = jnp.float32
AXES = ("dp", "fsdp")


def nt(a, b):
    return lax.dot_general(a, b, (((1,), (1,)), ((), ())), preferred_element_type=F32)


def nn(a, b):
    return lax.dot_general(a, b, (((1,), (0,)), ((), ())), preferred_element_type=F32)


def rows_at(i, n):
    return pl.ds(pl.multiple_of(i * n, n), n)


def fold8(x, op):
    return op(x.reshape(x.shape[0] // 8, 8, x.shape[1]), axis=0)


def select_slots(src, routes, lanes, dst_store):
    for half in range(2):
        r = [jnp.broadcast_to(routes[j : j + 1, :], (32, lanes)) for j in range(TOPK)]
        acc = [jnp.zeros((32, lanes), F32) for _ in range(TOPK)]
        for e in range(E):
            block = src(e * HD + half * 32)
            for j in range(TOPK):
                acc[j] = jnp.where(r[j] == e, block, acc[j])
        for j in range(TOPK):
            dst_store(j, half, acc[j])


def spread_slots(vals, routes, lanes, dst_store):
    for half in range(2):
        r = [jnp.broadcast_to(routes[j : j + 1, :], (32, lanes)) for j in range(TOPK)]
        v = [vals(j, half) for j in range(TOPK)]
        for e in range(E):
            acc = jnp.zeros((32, lanes), F32)
            for j in range(TOPK):
                acc = jnp.where(r[j] == e, v[j], acc)
            dst_store(e, half, acc.astype(BF))


def split_terms(x, n):
    terms = []
    for _ in range(n):
        t = x.astype(BF).astype(F32)
        terms.append(t)
        x = x - t
    return terms


def project_kernel(n_pieces, dst, length, tok, rt, *refs):
    pieces = refs[:n_pieces]
    (w1, normed_t, q_t, kv_t, ka, va, gate_t, misc, stat, ebias, w1_t, qa, psum, csum, eb) = refs[n_pieces:]
    at = 0
    for piece in pieces:
        for r in range(piece.shape[0]):
            w1[rows_at(dst[at + r], 16), :] = piece[r]
        at += piece.shape[0]
    for c in range(C1 // 128):
        w1_t[128 * c : 128 * (c + 1), :] = w1[:, 128 * c : 128 * (c + 1)].T
    misc[...] = w1_t[MISC:, :].astype(F32)
    lanes = lax.broadcasted_iota(jnp.int32, (16, 128), 1)
    for i in range(NB):
        tail = w1[16 * i : 16 * (i + 1), MISC:].astype(F32)
        for c in range(4):
            column = jnp.sum(jnp.where(lanes == VG + 5 + c, tail, 0.0), axis=1, keepdims=True)
            eb[64 * i + 16 * c : 64 * i + 16 * (c + 1), :] = jnp.broadcast_to(column, (16, 128))
    ebias[...] = eb[...].T[:8, :]
    gain, bias = misc[VG : VG + 1, :], misc[VG + 1 : VG + 2, :]
    psum[...] = jnp.zeros_like(psum)
    csum[...] = jnp.zeros_like(csum)
    n_valid = length[0]

    def block(b, carry):
        cols = rows_at(b, 256)
        x = tok[cols, :].astype(F32)
        center = x - jnp.mean(x, axis=-1, keepdims=True)
        var = jnp.mean(center * center, axis=-1, keepdims=True)
        normed = (center * lax.rsqrt(var + 1e-05) * gain + bias).astype(BF)
        n_t = normed.T
        normed_t[:, cols] = n_t
        qa[...] = nn(w1_t[...], n_t)
        kv_t[:, cols] = qa[QW : QW + 128, :].astype(BF)
        logits = qa[MISC : MISC + E, :]
        routes = rt[:, cols]
        for h in range(2):
            lane = slice(128 * h, 128 * h + 128)

            def store(j, half, acc, h=h):
                q_t[64 * j + 32 * half : 64 * j + 32 * half + 32, rows_at(2 * b + h, 128)] = acc.astype(BF)

            select_slots(
                lambda row, lane=lane: qa[row : row + 32, lane], routes[:, lane], 128, store
            )
        ids = lax.broadcasted_iota(jnp.int32, (E, 256), 0)
        valid = (lax.broadcasted_iota(jnp.int32, (1, 256), 1) + b * 256 < n_valid).astype(F32)
        picked = []
        hits = jnp.zeros((E, 256), F32)
        for j in range(TOPK):
            hit = ids == jnp.broadcast_to(routes[j : j + 1, :], (E, 256))
            picked.append(jnp.sum(jnp.where(hit, logits, 0.0), axis=0, keepdims=True))
            hits = hits + jnp.where(hit, 1.0, 0.0)
        picked = jnp.concatenate(picked, axis=0)
        expo = jnp.exp(picked - jnp.max(picked, axis=0, keepdims=True))
        gate_t[:, cols] = expo / jnp.sum(expo, axis=0, keepdims=True)
        expo = jnp.exp(logits - jnp.max(logits, axis=0, keepdims=True))
        probs = expo / jnp.sum(expo, axis=0, keepdims=True) * valid
        hits = hits * valid
        psum[...] += probs[:, :128] + probs[:, 128:]
        csum[...] += hits[:, :128] + hits[:, 128:]
        return carry

    lax.fori_loop(0, T // 256, block, 0)
    lane = lax.broadcasted_iota(jnp.int32, (T, 64), 1)
    slot = lax.broadcasted_iota(jnp.int32, (T, 64), 0)
    kv = kv_t[...].T
    mask = jnp.where(slot < n_valid, 0.0, NEG)
    ka[:, :64] = kv[:, :64]
    ka[:, 64:] = jnp.where(lane == 0, mask, jnp.where(lane < 4, 1.0, 0.0)).astype(BF)
    va[:, :64] = kv[:, 64:]
    va[:, 64:] = jnp.where(lane < 2, 1.0, 0.0).astype(BF)
    counts = jnp.sum(csum[...], axis=1, keepdims=True)
    probs = jnp.floor(jnp.sum(psum[...], axis=1, keepdims=True) * 128.0 + 0.5)
    lanes = lax.broadcasted_iota(jnp.int32, (E, 128), 1)
    tile = jnp.zeros((E, 128), F32)
    for value, first, digits in ((counts, 0, 4), (probs, 4, 6)):
        for k in range(digits):
            rest = jnp.floor(value * 0.125)
            tile = jnp.where(lanes == ST + first + k, value - 8.0 * rest, tile)
            value = rest
    low = jnp.concatenate([tile[16:, :], jnp.zeros((8, 128), F32)], axis=0)
    stat[...] = tile[:16, :] + pltpu.roll(low, 10, axis=1)


def attend_kernel(lo, hi, q_t, ka, kv_t, gate_t, rt, mix_t, lse, sp_t, q_s, s_s, acc_s):
    row = lax.broadcasted_iota(jnp.int32, (64, 1024), 0)
    q_s[64:, :] = jnp.where(row == 0, 1.0, 0.0).astype(BF)

    def block(b, carry):
        cols = rows_at(b, 128)
        own = rows_at(b - lo, 128)
        for j in range(TOPK):
            q_s[:64, 128 * j : 128 * (j + 1)] = q_t[64 * j : 64 * (j + 1), cols]
        full = b // 2

        def scores(c, m):
            s = nn(ka[rows_at(c, 256), :], q_s[...])
            s_s[rows_at(c, 256), :] = s
            return jnp.maximum(m, fold8(s, jnp.max))

        m = lax.fori_loop(0, full, scores, jnp.full((8, 1024), NEG, F32))
        s = nn(ka[rows_at(full, 256), :], q_s[...])
        at_s = lax.broadcasted_iota(jnp.int32, (256, 1024), 0) + full * 256
        at_t = (lax.broadcasted_iota(jnp.int32, (256, 1024), 1) & 127) + b * 128
        s = jnp.where(at_s <= at_t, s, NEG)
        s_s[rows_at(full, 256), :] = s
        m = jnp.max(jnp.maximum(m, fold8(s, jnp.max)), axis=0, keepdims=True)
        acc_s[...] = jnp.zeros_like(acc_s)

        def values(c, total):
            e = jnp.exp2((s_s[rows_at(c, 256), :] - m) * SCALE2)
            acc_s[...] += nn(kv_t[64:, rows_at(c, 256)], e.astype(BF))
            return total + fold8(e, jnp.sum)

        total = lax.fori_loop(0, full + 1, values, jnp.zeros((8, 1024), F32))
        total = jnp.sum(total, axis=0, keepdims=True)
        top = m + jnp.log(total) * HD**0.5
        inv = 1.0 / total
        for j in range(TOPK):
            lane = slice(128 * j, 128 * (j + 1))
            lse[j : j + 1, own] = top[:, lane]
            mix_t[64 * j : 64 * (j + 1), own] = acc_s[:, lane] * inv[:, lane]
        gate = gate_t[:, cols]

        def vals(j, half):
            at = 64 * j + 32 * half
            return mix_t[at : at + 32, own] * gate[j : j + 1, :]

        def store(e, half, block):
            at = 64 * e + 32 * half
            sp_t[at : at + 32, own] = block

        spread_slots(vals, rt[:, cols], 128, store)
        return carry

    lax.fori_loop(lo, hi, block, 0)


def join(parts, whole):
    at = 0
    for part in parts:
        whole[:, at : at + part.shape[1]] = part[...]
        at += part.shape[1]


def ffn_kernel(n_pieces, n_parts, dst, tok, cot, vec, ebias, *refs):
    pieces, parts = refs[:n_pieces], refs[n_pieces : n_pieces + n_parts]
    (out, middle, dexp, wo, we, sp_t, sends, keeps, rsum, ebg, wr, act, n2_t, grad) = refs[
        n_pieces + n_parts :
    ]
    join(parts, sp_t)
    at = 0
    for piece in pieces:
        for r in range(piece.shape[0]):
            i = dst[at + r]
            for q in range(3):
                wo[rows_at(3 * i + q, 16), :] = piece[r, :, 512 * q : 512 * (q + 1)]
            we[rows_at(i, 16), :] = piece[r, :, 1536 : 1536 + FF]
            for q in range(4):
                wr[rows_at(4 * i + q, 16), :] = piece[
                    r, :, 1536 + FF + 512 * q : 1536 + FF + 512 * (q + 1)
                ]
        at += piece.shape[0]
    gain, bias = vec[VG + 2 : VG + 3, :], vec[VG + 3 : VG + 4, :]
    rbias = vec[VG + 4 : VG + 5, :]
    ebg[...] = jnp.zeros_like(ebg)
    rsum[...] = jnp.zeros_like(rsum)
    c0, c1 = math.sqrt(2.0 / math.pi), 0.044715

    def block(b, carry):
        rows = rows_at(b, 256)
        mid = tok[rows, :].astype(F32) + nn(sp_t[:, rows].T, wo[...])
        middle[rows, :] = mid
        center = mid - jnp.mean(mid, axis=-1, keepdims=True)
        var = jnp.mean(center * center, axis=-1, keepdims=True)
        n2 = (center * lax.rsqrt(var + 1e-05) * gain + bias).astype(BF)
        n2_t[:, rows] = n2.T
        dy = cot[rows, :]
        red = jnp.zeros((256, 512), F32)
        for f in range(FF // 512):
            fs = slice(512 * f, 512 * (f + 1))
            u = nn(n2, we[:, fs]) + ebias[0:1, fs]
            da = nt(dy, wr[fs, :])
            sq = u * u
            th = jnp.tanh(c0 * u * (1.0 + c1 * sq))
            half = 0.5 * (1.0 + th)
            a = (u * half).astype(BF)
            act[rows, fs] = a
            red = red + nn(a, wr[fs, :])
            slope = half + 0.5 * u * (1.0 - th * th) * (c0 * (1.0 + 3.0 * c1 * sq))
            g = (da * slope).astype(BF)
            dexp[rows, fs] = g
            ebg[:, fs] += fold8(g.astype(F32), jnp.sum)
        out[rows, :] = (mid + (red + rbias)).astype(BF)
        rsum[...] += fold8(dy.astype(F32), jnp.sum)
        return carry

    lax.fori_loop(0, T // 256, block, 0)

    def reduce_grad(f, carry):
        grad[rows_at(f, 256), :] = nn(act[:, rows_at(f, 256)].T, cot[...]).astype(BF)
        return carry

    lax.fori_loop(0, FF // 256, reduce_grad, 0)
    for r in range(NB):
        i = dst[r]
        ref = keeps if r < NB // 2 else sends
        for q in range(4):
            ref[r % (NB // 2), :, FF + 512 * q : FF + 512 * (q + 1)] = grad[rows_at(4 * i + q, 16), :]
    for f in range(4):
        grad[512 * f : 512 * (f + 1), :] = nn(n2_t[...], dexp[:, 512 * f : 512 * (f + 1)]).astype(BF)
    for r in range(NB):
        i = dst[r]
        ref = keeps if r < NB // 2 else sends
        for f in range(4):
            ref[r % (NB // 2), :, 512 * f : 512 * (f + 1)] = grad[rows_at(32 * f + i, 16), :]


def middle_kernel(n_parts, dst, cot, middle, dexp, wo, we, sp_t, gate_t, rt, vec, *refs):
    (mgrad, gm_t, delta, dl_t, sends, keeps, vsum, low, sg, grad, mix_t) = refs[n_parts:]
    join(refs[:n_parts], mix_t)
    gain = vec[VG + 2 : VG + 3, :]
    vsum[...] = jnp.zeros_like(vsum)
    dl_t[...] = jnp.zeros_like(dl_t)

    def block(b, carry):
        rows = rows_at(b, 256)
        h = nt(dexp[rows, :], we[...])
        mid = middle[rows, :]
        center = mid - jnp.mean(mid, axis=-1, keepdims=True)
        var = jnp.mean(center * center, axis=-1, keepdims=True)
        r = lax.rsqrt(var + 1e-05)
        n = center * r
        vsum[0:8, :] += fold8(h * n, jnp.sum)
        vsum[8:16, :] += fold8(h, jnp.sum)
        k = h * gain
        inner = r * (
            k - jnp.mean(k, axis=-1, keepdims=True) - n * jnp.mean(k * n, axis=-1, keepdims=True)
        )
        mg = cot[rows, :].astype(F32) + inner
        mgrad[rows, :] = mg
        ag = mg.astype(BF)
        low[rows, :] = ag
        sg[...] = nt(wo[...], ag)
        for h2 in range(2):
            cols = rows_at(2 * b + h2, 128)
            lane = slice(128 * h2, 128 * h2 + 128)
            routes = rt[:, cols]
            gate = gate_t[:, cols]
            gg = [0.0] * TOPK
            dd = [0.0] * TOPK

            def store(j, half, acc, cols=cols, gate=gate, gg=gg, dd=dd):
                at = 64 * j + 32 * half
                m = (acc * gate[j : j + 1, :]).astype(BF)
                gm_t[at : at + 32, cols] = m
                mixed = mix_t[at : at + 32, cols]
                gg[j] = gg[j] + jnp.sum(mixed * acc, axis=0, keepdims=True)
                dd[j] = dd[j] + jnp.sum(mixed * m.astype(F32), axis=0, keepdims=True)

            select_slots(lambda row, lane=lane: sg[row : row + 32, lane], routes, 128, store)
            gg = jnp.concatenate(gg, axis=0)
            delta[:, cols] = jnp.concatenate(dd, axis=0)
            lg = gate * (gg - jnp.sum(gate * gg, axis=0, keepdims=True))
            ids = lax.broadcasted_iota(jnp.int32, (E, 128), 0)
            dl = jnp.zeros((E, 128), F32)
            for j in range(TOPK):
                hit = ids == jnp.broadcast_to(routes[j : j + 1, :], (E, 128))
                dl = jnp.where(hit, jnp.broadcast_to(lg[j : j + 1, :], (E, 128)), dl)
            dl_t[:32, cols] = jnp.concatenate([dl, jnp.zeros((8, 128), F32)], axis=0).astype(BF)
        return carry

    lax.fori_loop(0, T // 256, block, 0)

    def output_grad(f, carry):
        grad[rows_at(f, 256), :] = nn(sp_t[rows_at(f, 256), :], low[...]).astype(BF)
        return carry

    lax.fori_loop(0, QW // 256, output_grad, 0)
    for r in range(NB):
        i = dst[r]
        ref = keeps if r < NB // 2 else sends
        for q in range(3):
            ref[r % (NB // 2), :, 512 * q : 512 * (q + 1)] = grad[rows_at(3 * i + q, 16), :]


def attend_back_kernel(lo, hi, first, n_parts, q_t, gm_t, ka, va, kv_t, delta, rt, *refs):
    dq_out, dkv_out, q_s, g_s, dq_s, lse = refs[-6:]
    join(refs[:n_parts], lse)
    row = lax.broadcasted_iota(jnp.int32, (64, 1024), 0)
    dkv_out[...] = jnp.zeros((T, 128), F32) if first else refs[n_parts][...]

    def block(b, carry):
        cols = rows_at(b, 128)
        for j in range(TOPK):
            lane = slice(128 * j, 128 * (j + 1))
            q_s[:64, lane] = q_t[64 * j : 64 * (j + 1), cols]
            g_s[:64, lane] = gm_t[64 * j : 64 * (j + 1), cols]
            rows = row[:, :128]
            tail = jnp.where(rows == 0, 1.0, 0.0)
            for k, term in enumerate(split_terms(-lse[j : j + 1, cols], 3)):
                tail = jnp.where(rows == k + 1, jnp.broadcast_to(term, (64, 128)), tail)
            q_s[64:, lane] = tail.astype(BF)
            tail = jnp.zeros((64, 128), F32)
            for k, term in enumerate(split_terms(-delta[j : j + 1, cols], 2)):
                tail = jnp.where(rows == k, jnp.broadcast_to(term, (64, 128)), tail)
            g_s[64:, lane] = tail.astype(BF)
        dq_s[...] = jnp.zeros_like(dq_s)
        full = b // 2

        def chunk(c, diagonal):
            at = rows_at(c, 256)
            e = jnp.exp2(nn(ka[at, :], q_s[...]) * SCALE2)
            if diagonal:
                at_s = lax.broadcasted_iota(jnp.int32, (256, 1024), 0) + c * 256
                at_t = (lax.broadcasted_iota(jnp.int32, (256, 1024), 1) & 127) + b * 128
                e = jnp.where(at_s <= at_t, e, 0.0)
            ds = (e * nn(va[at, :], g_s[...])).astype(BF)
            dq_s[...] += nn(kv_t[:64, at], ds)
            dkv_out[at, :64] += nt(ds, q_s[:64, :])
            dkv_out[at, 64:] += nt(e.astype(BF), g_s[:64, :])

        def step(c, carry):
            chunk(c, False)
            return carry

        lax.fori_loop(0, full, step, 0)
        chunk(full, True)

        def vals(j, half):
            return dq_s[32 * half : 32 * half + 32, 128 * j : 128 * (j + 1)] * HD**-0.5

        out_cols = rows_at(b - lo, 128)

        def store(e, half, block):
            at = 64 * e + 32 * half
            dq_out[at : at + 32, out_cols] = block

        spread_slots(vals, rt[:, cols], 128, store)
        return carry

    lax.fori_loop(lo, hi, block, 0)


def query_grad_kernel(n_parts, dst, dkv, dl_t, normed_t, w1, vsum, rsum, ebg, stat, *refs):
    parts = refs[:n_parts]
    dy_t, sends, keeps, grad, vecs, ysum, eb = refs[n_parts:]
    join(parts, dy_t.at[:QW])
    lane = lax.broadcasted_iota(jnp.int32, (T, 128), 1)
    kv = (dkv[...] * jnp.where(lane < 64, HD**-0.5, 1.0)).astype(BF)
    dy_t[QW:MISC, :] = kv.T
    dy_t[MISC:, :] = dl_t[...]
    cross = jnp.zeros((D, 1), F32)
    for c in range(C1 // 256):
        cs = slice(256 * c, 256 * (c + 1))
        g = nt(normed_t[...], dy_t[cs, :])
        grad[:, cs] = g
        cross = cross + jnp.sum(w1[:, cs].astype(F32) * g, axis=1, keepdims=True)
        total = dy_t[cs, 0:128].astype(F32)
        for k in range(1, T // 128):
            total = total + dy_t[cs, 128 * k : 128 * (k + 1)].astype(F32)
        ysum[cs, :] = total.astype(BF)
    vecs[...] = jnp.zeros_like(vecs)
    total = lambda x: jnp.sum(x, axis=0, keepdims=True)
    vecs[VG + 2 : VG + 3, :] = total(vsum[0:8, :])
    vecs[VG + 3 : VG + 4, :] = total(vsum[8:16, :])
    vecs[VG + 4 : VG + 5, :] = total(rsum[...])
    eb[...] = jnp.broadcast_to(total(ebg[...]), (128, FF)).T
    lanes = lax.broadcasted_iota(jnp.int32, (D, 128), 1)
    bias_grad = jnp.sum(nn(w1[...], ysum[...]), axis=1, keepdims=True)
    tail = w1[:, MISC:].astype(F32)
    gain = jnp.sum(jnp.where(lanes == VG, tail, 0.0), axis=1, keepdims=True)
    bias = jnp.sum(jnp.where(lanes == VG + 1, tail, 0.0), axis=1, keepdims=True)
    gain_grad = (cross - bias * bias_grad) / gain
    grad[:, MISC:] += (
        vecs[...].T + jnp.where(lanes == VG, gain_grad, 0.0) + jnp.where(lanes == VG + 1, bias_grad, 0.0)
    )
    for r in range(NB):
        i = dst[r]
        ref = keeps if r < NB // 2 else sends
        ref[r % (NB // 2), :, :MISC] = grad[rows_at(i, 16), :MISC].astype(BF)
        tail = grad[rows_at(i, 16), MISC:] + stat[...]
        for c in range(4):
            tail = tail + jnp.where(lanes[:16] == VG + 5 + c, eb[rows_at(4 * i + c, 16), :], 0.0)
        ref[r % (NB // 2), :, MISC:] = tail.astype(BF)


def input_grad_kernel(w1, dy_t, tok, mgrad, vec, out):
    gain = vec[VG : VG + 1, :]

    def block(b, carry):
        rows = rows_at(b, 256)
        h = nn(w1[...], dy_t[:, rows]).T
        x = tok[rows, :].astype(F32)
        center = x - jnp.mean(x, axis=-1, keepdims=True)
        var = jnp.mean(center * center, axis=-1, keepdims=True)
        r = lax.rsqrt(var + 1e-05)
        n = center * r
        k = h * gain
        inner = r * (
            k - jnp.mean(k, axis=-1, keepdims=True) - n * jnp.mean(k * n, axis=-1, keepdims=True)
        )
        out[rows, :] = (mgrad[rows, :] + inner).astype(BF)
        return carry

    lax.fori_loop(0, T // 256, block, 0)


SMEM = pltpu.SMEM
VMEM = pltpu.VMEM


def call(kernel, smem, args, outs, scratch=(), flops=0, after=(), smem_outs=0):
    specs = [pl.BlockSpec(memory_space=SMEM)] * smem
    specs += [pl.BlockSpec(memory_space=VMEM)] * (len(args) - smem)
    specs += [pl.BlockSpec(memory_space=pl.ANY)] * len(after)
    n_args = len(args)
    total = sum(math.prod(a.shape) * a.dtype.itemsize for a in args)
    total += sum(math.prod(s) * jnp.dtype(d).itemsize for s, d in outs)
    return pl.pallas_call(
        lambda *refs: kernel(*refs[:n_args], *refs[n_args + len(after) :]),
        out_shape=[jax.ShapeDtypeStruct(s, d) for s, d in outs],
        in_specs=specs,
        out_specs=[pl.BlockSpec(memory_space=VMEM)] * (len(outs) - smem_outs)
        + [pl.BlockSpec(memory_space=SMEM)] * smem_outs,
        scratch_shapes=[VMEM(s, d) for s, d in scratch],
        compiler_params=pltpu.CompilerParams(vmem_limit_bytes=60 * 1024 * 1024),
        cost_estimate=pl.CostEstimate(flops=flops, bytes_accessed=total, transcendentals=0),
    )(*args, *after)


def project(dst, length, tok, rt, pieces, after):
    return call(
        functools.partial(project_kernel, len(pieces)),
        2,
        (dst, length, tok, rt, *pieces),
        [
            ((D, C1), BF), ((D, T), BF), ((TOPK * HD, T), BF), ((128, T), BF), ((T, 128), BF), ((T, 128), BF),
            ((TOPK, T), F32), ((128, D), F32), ((16, 128), F32), ((8, FF), F32),
        ],
        [((C1, D), BF), ((C1, 256), F32), ((E, 128), F32), ((E, 128), F32), ((FF, 128), F32)],
        flops=2 * T * D * C1,
        after=after,
    )


def attend(lo, hi, q_t, ka, kv_t, gate_t, rt, after):
    n = 128 * (hi - lo)
    return call(
        functools.partial(attend_kernel, lo, hi),
        0,
        (q_t, ka, kv_t, gate_t, rt),
        [((TOPK * HD, n), F32), ((TOPK, n), F32), ((QW, n), BF)],
        [((128, 1024), BF), ((T, 1024), F32), ((64, 1024), F32)],
        flops=8 * TOPK * T * T * HD,
        after=after,
    )


def ffn(dst, tok, cot, vec, ebias, pieces, parts):
    half = NB // 2
    return call(
        functools.partial(ffn_kernel, len(pieces), len(parts)),
        1,
        (dst, tok, cot, vec, ebias, *pieces, *parts),
        [
            ((T, D), BF), ((T, D), F32), ((T, FF), BF), ((QW, D), BF), ((D, FF), BF), ((QW, T), BF),
            ((half, 16, 2 * FF), BF), ((half, 16, 2 * FF), BF), ((8, D), F32), ((8, FF), F32),
        ],
        [((FF, D), BF), ((T, FF), BF), ((D, T), BF), ((FF, D), BF)],
        flops=2 * T * D * (5 * FF + QW),
    )


def middle_back(dst, cot, middle, dexp, wo, we, sp_t, gate_t, rt, vec, mixed):
    half = NB // 2
    return call(
        functools.partial(middle_kernel, len(mixed)),
        1,
        (dst, cot, middle, dexp, wo, we, sp_t, gate_t, rt, vec, *mixed),
        [
            ((T, D), F32), ((TOPK * HD, T), BF), ((TOPK, T), F32), ((128, T), BF),
            ((half, 16, QW), BF), ((half, 16, QW), BF), ((16, D), F32),
        ],
        [((T, D), BF), ((QW, 256), F32), ((QW, D), BF), ((TOPK * HD, T), F32)],
        flops=2 * T * D * (FF + 2 * QW),
    )


def attend_back(lo, hi, q_t, gm_t, ka, va, kv_t, delta, rt, lse, dkv, after):
    return call(
        functools.partial(attend_back_kernel, lo, hi, dkv is None, len(lse)),
        0,
        (q_t, gm_t, ka, va, kv_t, delta, rt, *lse) + (() if dkv is None else (dkv,)),
        [((QW, 128 * (hi - lo)), BF), ((T, 128), F32)],
        [((128, 1024), BF), ((128, 1024), BF), ((64, 1024), F32), ((TOPK, T), F32)],
        flops=8 * TOPK * T * T * HD,
        after=after,
    )


def query_grads(dst, dkv, dl_t, normed_t, w1, vsum, rsum, ebg, stat, parts, after):
    half = NB // 2
    return call(
        functools.partial(query_grad_kernel, len(parts)),
        1,
        (dst, dkv, dl_t, normed_t, w1, vsum, rsum, ebg, stat, *parts),
        [((C1, T), BF), ((half, 16, C1), BF), ((half, 16, C1), BF)],
        [((D, C1), F32), ((128, D), F32), ((C1, 128), BF), ((FF, 128), F32)],
        flops=2 * T * D * C1,
        after=after,
    )


def input_grad(w1, dy_t, tok, mgrad, vec, after):
    return call(
        input_grad_kernel,
        0,
        (w1, dy_t, tok, mgrad, vec),
        [((T, D), BF)],
        flops=2 * T * D * C1,
        after=after,
    )[0]


def finish_ffn_kernel(keep, recv, expand, reduce):
    total = keep[0].astype(F32) + recv[0].astype(F32)
    expand[...] = total[:, :FF]
    for q in range(4):
        reduce[16 * q : 16 * (q + 1), :] = total[:, FF + 512 * q : FF + 512 * (q + 1)]


def finish_output_kernel(keep, recv, output):
    total = keep[0].astype(F32) + recv[0].astype(F32)
    for q in range(3):
        output[16 * q : 16 * (q + 1), :] = total[:, 512 * q : 512 * (q + 1)]


def finish_query_kernel(keep, recv, query, key_value, router, stats, fg, fb, sg, sb, rb, eb):
    total = keep[0].astype(F32) + recv[0].astype(F32)
    query[...] = total[:, :QW]
    key_value[...] = total[:, QW:MISC]
    router[...] = total[:, MISC : MISC + E]
    tail = jnp.concatenate([total[:, MISC:], jnp.zeros((112, 128), F32)], axis=0).T
    for k, ref in enumerate((fg, fb, sg, sb, rb)):
        ref[...] = tail[VG + k : VG + k + 1, :16]
    for c in range(4):
        eb[:, 16 * c : 16 * (c + 1)] = tail[VG + 5 + c : VG + 6 + c, :16]
    stats[...] = statistics(tail[ST : ST + 24, :])


def statistics(digits):
    counts, probs = jnp.zeros((1, 128), F32), jnp.zeros((1, 128), F32)
    for k in range(10):
        row = digits[k : k + 1, :] + pltpu.roll(digits[k + 10 : k + 11, :], 16, axis=1)
        if k < 4:
            counts = counts + row * 8.0**k
        else:
            probs = probs + row * 8.0 ** (k - 4)
    valid_total = jnp.sum(counts, axis=1, keepdims=True) / TOPK
    counts = E * counts / (TOPK * valid_total)
    probs = E * (probs / 128.0) / valid_total
    return jnp.concatenate([counts[:, :E], probs[:, :E]], axis=0)


def statistics_kernel(digits, stats):
    stats[...] = statistics(digits[...])


def finish(kernel, pair, outs):
    return call(kernel, 0, pair, [(s, F32) for s in outs])


MASKS = ((2, 4, 8, 16), (4, 2, 16, 8))
CORE = 1


def far(core, r):
    return sum(m for k, m in enumerate(MASKS[core]) if r >> k & 1)


def swap(x, step):
    perm = [(i, i ^ (CORE if step == 4 else MASKS[i & 1][step])) for i in range(32)]
    return lax.ppermute(x, AXES, perm)


def widen(held, step):
    return jnp.concatenate([held, swap(held, step)], axis=0)


def tie(x, *others):
    return lax.optimization_barrier((x, *others))[0]


def add(a, b):
    return (a.astype(F32) + b.astype(F32)).astype(BF)


def narrow(keep, recv):
    half = keep.shape[0] // 2
    send = add(keep[half:], recv[half:])
    return add(keep[:half], recv[:half]), send


def pack_kernel(
    paired, qw, kvw, rw, ow, ew, rw2, routes, fg, fb, sg, sb, rb, eb, one, two, rt, table, cols
):
    me = lax.axis_index(AXES)
    core = me & 1
    for r in range(16):
        if paired:
            near = jnp.where(core == 0, far(0, r), far(1, r))
            across = jnp.where(core == 0, far(1, r), far(0, r))
            table[r] = me ^ near
            table[16 + r] = me ^ CORE ^ across
        else:
            table[r] = r
            table[16 + r] = 16 + r
    rt[...] = routes[...].T
    if not paired:
        return
    cols[...] = jnp.zeros_like(cols)
    for k, ref in enumerate((fg, fb, sg, sb, rb)):
        cols[VG + k : VG + k + 1, :16] = ref[...].astype(F32)
    for c in range(4):
        cols[VG + 5 + c : VG + 6 + c, :16] = eb[:, 16 * c : 16 * (c + 1)].astype(F32)
    cols[:E, :16] = rw[...].astype(F32).T
    one[0, :, :QW] = qw[...]
    one[0, :, QW:MISC] = kvw[...]
    one[0, :, MISC:] = cols[...].T[:16, :].astype(BF)
    for q in range(3):
        two[0, :, 512 * q : 512 * (q + 1)] = ow[16 * q : 16 * (q + 1), :]
    two[0, :, 1536 : 1536 + FF] = ew[...]
    for q in range(4):
        two[0, :, 1536 + FF + 512 * q : 1536 + FF + 512 * (q + 1)] = rw2[16 * q : 16 * (q + 1), :]


def per_device(
    n_devices, tokens, lengths, routes, query_weight, key_value_weight, router_weight, output_weight,
    expand_weight, expand_bias, reduce_weight, reduce_bias, first_gain, first_bias, second_gain,
    second_bias, cotangent,
):
    paired = n_devices == NB
    tok, cot = tokens[0], cotangent[0]
    vectors = [first_gain, first_bias, second_gain, second_bias, reduce_bias, expand_bias]
    one, two, rt, table = call(
        functools.partial(pack_kernel, paired),
        0,
        (
            query_weight, key_value_weight, router_weight, output_weight, expand_weight, reduce_weight,
            routes[0], *[v.reshape(1, -1) for v in vectors],
        ),
        [((1, 16, C1), BF), ((1, 16, C2), BF), ((TOPK, T), jnp.int32), ((NB,), jnp.int32)],
        [((128, 128), F32)],
        smem_outs=1,
    )
    if paired:
        one = widen(widen(one, 0), 1)
        two = tie(two, one)
        one = widen(one, 2)
        two = tie(widen(two, 0), one)
        one = widen(one, 3)
        two = tie(widen(two, 1), one)
        pieces_one = [one, swap(one, 4)]
        after, coming = [two], swap(two, 2)
    else:
        gather = lambda w: lax.all_gather(w, AXES, axis=0, tiled=True)
        blocks = lambda w: w.reshape(NB, -1, 16, 512).transpose(0, 2, 1, 3).reshape(NB, 16, -1)
        columns = jnp.stack(vectors[:5], axis=1)
        fill = jnp.zeros((columns.shape[0], 128 - E - 5), BF)
        first = jnp.concatenate([query_weight, key_value_weight, router_weight, columns, fill], axis=1)
        pieces_one = [gather(first).reshape(NB, 16, C1)]
        parts = [blocks(gather(output_weight)), gather(expand_weight).reshape(NB, 16, FF)]
        pieces_two = [jnp.concatenate(parts + [blocks(gather(reduce_weight))], axis=2)]
        after = []

    w1, normed_t, q_t, kv_t, ka, va, gate_t, vec, stat, ebias = project(
        table, lengths, tok, rt, pieces_one, after
    )
    if not paired:
        ebias = jnp.broadcast_to(gather(expand_bias).astype(F32), (8, FF))
    mixed, lse, spread = [], [], []
    done = stat
    for step, (lo, hi) in zip((3, 4), ((0, 6), (6, 8))):
        if paired:
            two = jnp.concatenate([two, tie(coming, done)], axis=0)
            after, coming = [two], swap(two, step)
        m, top, sp = attend(lo, hi, q_t, ka, kv_t, gate_t, rt, after)
        mixed.append(m)
        lse.append(top)
        spread.append(sp)
        done = top
    if paired:
        pieces_two = [two, tie(coming, done)]
    out, middle, dexp, wo, we, sp_t, sends, keeps, rsum, ebg = ffn(
        table, tok, cot, vec, ebias, pieces_two, spread
    )
    ffn_sum = (keeps, sends)
    mgrad, gm_t, delta, dl_t, sends, keeps, vsum = middle_back(
        table, cot, middle, dexp, wo, we, sp_t, gate_t, rt, vec, mixed
    )
    output_sum = (keeps, sends)
    dkv, parts = None, []
    if paired:
        after = ffn_sum = narrow(ffn_sum[0], tie(swap(ffn_sum[1], 4), delta))
        steps = ((3, 4), (2, 3), (1, 2))
    else:
        after, steps = (), (None,) * 3
    for (lo, hi), step in zip(((0, 4), (4, 6), (6, 8)), steps):
        dq, dkv = attend_back(lo, hi, q_t, gm_t, ka, va, kv_t, delta, rt, lse, dkv, after)
        parts.append(dq)
        if paired:
            ffn_sum = narrow(ffn_sum[0], tie(swap(ffn_sum[1], step[0]), dkv))
            output_sum = narrow(output_sum[0], tie(swap(output_sum[1], step[1]), dkv))
            after = (*ffn_sum, *output_sum)
    dy_t, sends, keeps = query_grads(
        table, dkv, dl_t, normed_t, w1, vsum, rsum, ebg, stat, parts, after
    )
    query_sum = (keeps, sends)
    if paired:
        ffn_sum = (ffn_sum[0], tie(swap(ffn_sum[1], 0), sends))
        output_sum = narrow(output_sum[0], tie(swap(output_sum[1], 1), sends))
        query_sum = narrow(keeps, swap(tie(sends, ffn_sum[1], *output_sum), 4))
        after = query_sum
    tokens_grad = input_grad(w1, dy_t, tok, mgrad, vec, after)

    if paired:
        output_sum = (output_sum[0], swap(output_sum[1], 0))
        query_sum = (query_sum[0], tie(swap(query_sum[1], 3), tokens_grad))
        for step in (2, 1, 0):
            keep, send = narrow(*query_sum)
            query_sum = (keep, swap(send, step))
        expand_grad, reduce_grad = finish(finish_ffn_kernel, ffn_sum, [(16, FF), (64, D)])
        (output_grad,) = finish(finish_output_kernel, output_sum, [(48, D)])
        query_grad, key_value_grad, router_grad, router_stats, *rest = finish(
            finish_query_kernel,
            query_sum,
            [(16, QW), (16, 128), (16, E), (2, E)] + [(1, 16)] * 5 + [(1, 64)],
        )
        fg, fb, sg, sb, rb, expand_bias_grad = [g.reshape(-1) for g in rest]
    else:
        whole = lambda pair: jnp.concatenate(pair, axis=0)
        scatter = lambda g: lax.psum_scatter(g, AXES, scatter_dimension=0, tiled=True)
        rows_of = lambda g, n: g.reshape(NB, 16, n, 512).transpose(0, 2, 1, 3).reshape(NB * 16 * n, 512)
        g = whole(ffn_sum).astype(F32)
        expand_grad = scatter(g[:, :, :FF].reshape(D, FF))
        reduce_grad = scatter(rows_of(g[:, :, FF:], 4))
        output_grad = scatter(rows_of(whole(output_sum).astype(F32), 3))
        g = whole(query_sum).astype(F32).reshape(D, C1)
        query_grad, key_value_grad = scatter(g[:, :QW]), scatter(g[:, QW:MISC])
        router_grad = scatter(g[:, MISC : MISC + E])
        fg, fb, sg, sb, rb = [scatter(g[:, MISC + VG + k]) for k in range(5)]
        expand_bias_grad = scatter(jnp.sum(ebg, axis=0))
        digits = jnp.pad(lax.psum(stat[:, ST : ST + 24], AXES).T, ((0, 0), (0, 112)))
        (router_stats,) = call(statistics_kernel, 0, (digits,), [((2, E), F32)])
    return (
        out[None], tokens_grad[None], query_grad, key_value_grad, router_grad, output_grad, expand_grad,
        expand_bias_grad, reduce_grad, rb, fg, fb, sg, sb, router_stats,
    )


def solution(mesh):
    both = lambda n: P(AXES, *([None] * (n - 1)))
    in_specs = tuple(both(n) for n in (3, 1, 3, 2, 2, 2, 2, 2, 1, 2, 1, 1, 1, 1, 1, 3))
    out_specs = tuple(both(n) for n in (3, 3, 2, 2, 2, 2, 2, 1, 2, 1, 1, 1, 1, 1)) + (P(),)
    return jax.shard_map(
        functools.partial(per_device, mesh.size),
        mesh=mesh,
        in_specs=in_specs,
        out_specs=out_specs,
        check_vma=False,
    )
```

time: 1530 us -> 234 us (0.15)
  waiting for transfers between devices: 639 us -> 39.5 us
  local copies, waits for them, and re-layouts: 415 us -> 12.2 us
  matrix products: 174 us -> 0 us
  blocking collectives: 160 us -> 0 us
  Pallas kernels: 0 us -> 138 us
  other arithmetic: 108 us -> 14 us
  starting transfers between devices: 0.86 us -> 27.7 us
  between operations: 17.1 us -> 1.65 us
    reduce_scatter x6 -> x0, waiting for transfers between devices: 636 us -> none  [the longest x1 144 us: per_device(): lax.psum_scatter(reduce_weight_grad, ('dp', 'fsdp'), scatter_dimension=0,...]
    gather x10 -> x0, local copies, waits for them, and re-layouts: 289 us -> none  [the longest x2 122 us: per_device(): slot_grad = jnp.take_along_axis(spread_grad, route_flat[:, :, None], axis=1)]
    dot_general x34 -> x0, matrix products: 174 us -> none  [the longest x4 26.5 us: masked_scores(): jnp.einsum('tjd,sd->tjs', query_block, key_rows, preferred_element_type=j...]
    pallas_call x0 -> x14, Pallas kernels: none -> 138 us  [call(): pl.pallas_call(lambda *refs: kernel(*refs[:n_args], *refs[n_args + len(af...]
    unnamed x2 -> x0, blocking collectives: 81.7 us -> none
    all_gather x2 -> x0, blocking collectives: 78.4 us -> none  [the longest x1 41.2 us: per_device(): lax.all_gather(router_weight, ('dp', 'fsdp'), axis=0, tiled=True)]
    unnamed x6 -> x0, other arithmetic: 43.7 us -> none
    dynamic_update_slice x4 -> x0, local copies, waits for them, and re-layouts: 41.2 us -> none  [attend_forward(): return lax.map(one_block, (query_seq, starts))]
  transfers between devices with their start and end apart: 10 -> 25, of which waited for: 6 -> 11; matrix products, arithmetic and copies ran while one was open for 26% -> 5% of each run, Pallas kernels for 0% -> 45%
where the time goes in v1:
time: 234 us; the launch traced here: 233 us
  Pallas kernels  138 us (59%)
  waiting for transfers between devices  39.5 us (17%)
  starting transfers between devices  27.7 us (12%)
  other arithmetic  14 us (6%)
  local copies, waits for them, and re-layouts  12.2 us (5%)
    pallas_call x14, Pallas kernels, call(): pl.pallas_call(lambda *refs: kernel(*refs[:n_args], *refs[n_args + len(af...  138 us
    ppermute x25, waiting for transfers between devices, swap(): return lax.ppermute(x, AXES, perm)  39.5 us
    ppermute x25, starting transfers between devices, swap(): return lax.ppermute(x, AXES, perm)  27.7 us
    convert_element_type x12, other arithmetic, add(): return (a.astype(F32) + b.astype(F32)).astype(BF)  12.2 us
    unnamed x53, local copies, waits for them, and re-layouts  9.89 us
  transfers between devices with their start and end apart: 25, of which 11 were waited for; matrix products, arithmetic and copies ran while one was open for 5% of the time, Pallas kernels for 45%

profile of v1, /device:TPU:0, one launch (start us, length us, event | category | flops | bytes accessed | tf_op | source)
XLA Modules:
  0.0 233.4 jit_solution(5496239502352935884)
XLA Ops:
  4.6 3.1 %collective-permute-start = (bf16[1,16,1792]{2,1,0:T(8,128)(2,1)}, bf16[1,16,1792]{2,1,0:T(8,128)(2,1)S(1)}, u32[]{:S(2)}, u32[]{:S(2)}) collective-permute-start(bf16[1,16,1792]{2,1,0:T(8,128)(2,1)} %get-tuple-element.92), channel_id=1, source_target_pairs={{0,2},{1,5},{2,0},{3,7},{4,6},{5,1},{6,4},{7,3},{8,10},{9,13},{10,... | collective-permute-start | bytes 172040 | tf_op jit(solution)/shard_map/ppermute | solution.py:662
  11.5 2.5 %collective-permute-start.1 = (bf16[2,16,1792]{2,1,0:T(8,128)(2,1)S(1)}, bf16[2,16,1792]{2,1,0:T(8,128)(2,1)S(1)}, u32[]{:S(2)}, u32[]{:S(2)}) collective-permute-start(bf16[2,16,1792]{2,1,0:T(8,128)(2,1)S(1)} %pad_maximum_fusion.2), channel_id=1, source_target_pairs={{0,4},{1,3},{2,6},{3,1},{4,0},{5,7},{6,2},{7,5},{8,12},{9,11},{10,... | collective-permute-start | bytes 344072 | tf_op jit(solution)/shard_map/ppermute | solution.py:662
  14.0 3.3 %collective-permute-done.1 = bf16[2,16,1792]{2,1,0:T(8,128)(2,1)S(1)} collective-permute-done((bf16[2,16,1792]{2,1,0:T(8,128)(2,1)S(1)}, bf16[2,16,1792]{2,1,0:T(8,128)(2,1)S(1)}, u32[]{:S(2)}, u32[]{:S(2)}) %collective-permute-start.1) | collective-permute-done | bytes 114720 | tf_op jit(solution)/shard_map/ppermute | solution.py:662
  20.8 3.5 %collective-permute-done.2 = bf16[4,16,1792]{2,1,0:T(8,128)(2,1)S(1)} collective-permute-done((bf16[4,16,1792]{2,1,0:T(8,128)(2,1)S(1)}, bf16[4,16,1792]{2,1,0:T(8,128)(2,1)S(1)}, u32[]{:S(2)}, u32[]{:S(2)}) %collective-permute-start.2) | collective-permute-done | bytes 229408 | tf_op jit(solution)/shard_map/ppermute | solution.py:662
  29.6 3.3 %collective-permute-done.3 = bf16[8,16,1792]{2,1,0:T(8,128)(2,1)S(1)} collective-permute-done((bf16[8,16,1792]{2,1,0:T(8,128)(2,1)S(1)}, bf16[8,16,1792]{2,1,0:T(8,128)(2,1)S(1)}, u32[]{:S(2)}, u32[]{:S(2)}) %collective-permute-start.3) | collective-permute-done | bytes 458784 | tf_op jit(solution)/shard_map/ppermute | solution.py:662
  33.0 6.6 %collective-permute-done.6 = bf16[2,16,5632]{2,1,0:T(8,128)(2,1)S(1)} collective-permute-done((bf16[2,16,5632]{2,1,0:T(8,128)(2,1)S(1)}, bf16[2,16,5632]{2,1,0:T(8,128)(2,1)S(1)}, u32[]{:S(2)}, u32[]{:S(2)}) %collective-permute-start.6) | collective-permute-done | bytes 360480 | tf_op jit(solution)/shard_map/ppermute | solution.py:662
  43.1 10.9 %shard_map.272 = (bf16[512,1792]{1,0:T(8,128)(2,1)}, bf16[512,1024]{1,0:T(8,128)(2,1)}, bf16[512,1024]{1,0:T(8,128)(2,1)}, bf16[128,1024]{1,0:T(8,128)(2,1)}, bf...) custom-call(s32[32]{0:T(128)} %get-tuple-element.90.refs_0_, ...), custom_call_target="tpu_custom_call" | custom-call | flops 1879048192 | bytes 8003716 | tf_op jit(solution)/shard_map/pallas_call | solution.py:498
  56.2 12.8 %shard_map.273 = (f32[512,768]{1,0:T(8,128)}, f32[8,768]{1,0:T(8,128)}, bf16[1536,768]{1,0:T(8,128)(2,1)}) custom-call(bf16[512,1024]{1,0:T(8,128)(2,1)} %get-tuple-element.101.refs_0_, bf16[1024,128]{1,0:T(8,128)(2,1)} %get-tuple-element.102.refs_1_.refs_2_, bf16[128,1024]{1,0:T(8,128)(2,1)} %get-tuple-element.103.refs_2_.refs_4_, ...), custom_call_target="tpu_custom_call" | custom-call | flops 4294967296 | bytes 5595136 | tf_op jit(solution)/shard_map/pallas_call | solution.py:498
  69.0 5.1 %collective-permute-done.8 = bf16[8,16,5632]{2,1,0:T(8,128)(2,1)S(1)} collective-permute-done((bf16[8,16,5632]{2,1,0:T(8,128)(2,1)S(1)}, bf16[8,16,5632]{2,1,0:T(8,128)(2,1)S(1)}, u32[]{:S(2)}, u32[]{:S(2)}) %collective-permute-start.8) | collective-permute-done | bytes 1441824 | tf_op jit(solution)/shard_map/ppermute | solution.py:662
  75.3 7.9 %shard_map.274 = (f32[512,256]{1,0:T(8,128)}, f32[8,256]{1,0:T(8,128)}, bf16[1536,256]{1,0:T(8,128)(2,1)}) custom-call(bf16[512,1024]{1,0:T(8,128)(2,1)} %get-tuple-element.101.refs_0_, bf16[1024,128]{1,0:T(8,128)(2,1)} %get-tuple-element.102.refs_1_.refs_2_, bf16[128,1024]{1,0:T(8,128)(2,1)} %get-tuple-element.103.refs_2_.refs_4_, ...), custom_call_target="tpu_custom_call" | custom-call | flops 4294967296 | bytes 2957312 | tf_op jit(solution)/shard_map/pallas_call | solution.py:498
  84.9 29.9 %shard_map.275 = (bf16[1024,512]{1,0:T(8,128)(2,1)}, f32[1024,512]{1,0:T(8,128)}, bf16[1024,2048]{1,0:T(8,128)(2,1)}, bf16[1536,512]{1,0:T(8,128)(2,1)}, bf16[51...) custom-call(s32[32]{0:T(128)} %get-tuple-element.90.refs_0_, ...), custom_call_target="tpu_custom_call" | custom-call | flops 12348030976 | bytes 29769856 | tf_op jit(solution)/shard_map/pallas_call | solution.py:498
  115.4 20.2 %shard_map.276 = (f32[1024,512]{1,0:T(8,128)}, bf16[512,1024]{1,0:T(8,128)(2,1)}, f32[8,1024]{1,0:T(8,128)}, bf16[128,1024]{1,0:T(8,128)(2,1)}, bf16[16,16,1536]...) custom-call(s32[32]{0:T(128)} %get-tuple-element.90.refs_0_, bf16[1024,512]{1,0:T(8,128)(2,1)} %bitcast.29, ...), custom_call_target="tpu_custom_call" | custom-call | flops 5368709120 | bytes 21627008 | tf_op jit(solution)/shard_map/pallas_call | solution.py:498
  135.6 3.3 %add_convert_fusion = (bf16[8,16,4096]{2,1,0:T(8,128)(2,1)S(1)}, bf16[8,16,4096]{2,1,0:T(8,128)(2,1)}) fusion(bf16[16,16,4096]{2,1,0:T(8,128)(2,1)} %collective-permute-done.10, bf16[16,16,4096]{2,1,0:T(8,128)(2,1)S(1)} %copy-done.3), kind=kLoop, calls=%fused_computation | loop fusion | flops 4194304 | bytes 6291456 | tf_op jit(solution)/shard_map/convert_element_type | solution.py:674
  139.9 11.0 %shard_map.277 = (bf16[1536,512]{1,0:T(8,128)(2,1)}, f32[1024,128]{1,0:T(8,128)}) custom-call(bf16[512,1024]{1,0:T(8,128)(2,1)} %get-tuple-element.101.refs_0_, bf16[512,1024]{1,0:T(8,128)(2,1)} %get-tuple-element.120.refs_1_, bf16[1024,128]{1,0:T(8,128)(2,1)} %get-tuple-element.102.refs_1_.refs_2_, bf16[1024,128]{1,0:T(8,128)(2,1)} %get-tuple-element.121.refs_3_, ...), custom_call_target="tpu_custom_call" | custom-call | flops 4294967296 | bytes 5079040 | tf_op jit(solution)/shard_map/pallas_call | solution.py:498
  155.6 9.9 %shard_map.278 = (bf16[1536,256]{1,0:T(8,128)(2,1)}, f32[1024,128]{1,0:T(8,128)}) custom-call(bf16[512,1024]{1,0:T(8,128)(2,1)} %get-tuple-element.101.refs_0_, bf16[512,1024]{1,0:T(8,128)(2,1)} %get-tuple-element.120.refs_1_, bf16[1024,128]{1,0:T(8,128)(2,1)} %get-tuple-element.102.refs_1_.refs_2_, bf16[1024,128]{1,0:T(8,128)(2,1)} %get-tuple-element.121.refs_3_, ...), custom_call_target="tpu_custom_call" | custom-call | flops 4294967296 | bytes 4816896 | tf_op jit(solution)/shard_map/pallas_call | solution.py:498
  169.0 12.0 %shard_map.279 = (bf16[1536,256]{1,0:T(8,128)(2,1)}, f32[1024,128]{1,0:T(8,128)}) custom-call(bf16[512,1024]{1,0:T(8,128)(2,1)} %get-tuple-element.101.refs_0_, bf16[512,1024]{1,0:T(8,128)(2,1)} %get-tuple-element.120.refs_1_, bf16[1024,128]{1,0:T(8,128)(2,1)} %get-tuple-element.102.refs_1_.refs_2_, bf16[1024,128]{1,0:T(8,128)(2,1)} %get-tuple-element.121.refs_3_, ...), custom_call_target="tpu_custom_call" | custom-call | flops 4294967296 | bytes 4816896 | tf_op jit(solution)/shard_map/pallas_call | solution.py:498
  181.7 2.2 collective-permute-start.18
  185.5 8.4 %shard_map.280 = (bf16[1792,1024]{1,0:T(8,128)(2,1)}, bf16[16,16,1792]{2,1,0:T(8,128)(2,1)}, bf16[16,16,1792]{2,1,0:T(8,128)(2,1)}) custom-call(s32[32]{0:T(128)} %get-tuple-element.90.refs_0_, f32[1024,128]{1,0:T(8,128)} %get-tuple-element.134.refs_1_, bf16[128,1024]{1,0:T(8,128)(2,1)} %get-tuple-element.135.refs_2_, ...), custom_call_target="tpu_custom_call" | custom-call | flops 1879048192 | bytes 12443776 | tf_op jit(solution)/shard_map/pallas_call | solution.py:498
  194.5 2.7 %collective-permute-done.19 = bf16[16,16,1792]{2,1,0:T(8,128)(2,1)S(1)} collective-permute-done((bf16[16,16,1792]{2,1,0:T(8,128)(2,1)}, bf16[16,16,1792]{2,1,0:T(8,128)(2,1)S(1)}, u32[]{:S(2)}, u32[]{:S(2)}) %collective-permute-start.19) | collective-permute-done | bytes 917536 | tf_op jit(solution)/shard_map/ppermute | solution.py:662
  200.1 8.3 %shard_map.281 = bf16[1024,512]{1,0:T(8,128)(2,1)} custom-call(bf16[512,1792]{1,0:T(8,128)(2,1)} %get-tuple-element.112.refs_4_.refs_0_, bf16[1792,1024]{1,0:T(8,128)(2,1)} %get-tuple-element.145.refs_1_, bf16[1024,512]{1,0:T(8,128)(2,1)} %bitcast.20, f32[1024,512]{1,0:T(8,128)} %get-tuple-element.146.refs_3_, ...), custom_call_target="tpu_custom_call" | custom-call | flops 1879048192 | bytes 9961472 | tf_op jit(solution)/shard_map/pallas_call | solution.py:498
  209.7 5.0 %collective-permute-done.21 = bf16[4,16,1792]{2,1,0:T(8,128)(2,1)S(1)} collective-permute-done((bf16[4,16,1792]{2,1,0:T(8,128)(2,1)S(1)}, bf16[4,16,1792]{2,1,0:T(8,128)(2,1)S(1)}, u32[]{:S(2)}, u32[]{:S(2)}) %collective-permute-start.21) | collective-permute-done | bytes 229408 | tf_op jit(solution)/shard_map/ppermute | solution.py:662
  214.8 2.3 collective-permute-start.22
  217.0 4.7 %collective-permute-done.22 = bf16[2,16,1792]{2,1,0:T(8,128)(2,1)S(1)} collective-permute-done((bf16[2,16,1792]{2,1,0:T(8,128)(2,1)S(1)}, bf16[2,16,1792]{2,1,0:T(8,128)(2,1)S(1)}, u32[]{:S(2)}, u32[]{:S(2)}) %collective-permute-start.22) | collective-permute-done | bytes 114720 | tf_op jit(solution)/shard_map/ppermute | solution.py:662
  224.4 2.7 %collective-permute-done.24.refs_1_ = bf16[1,16,1536]{2,1,0:T(8,128)(2,1)S(1)} collective-permute-done((bf16[1,16,1536]{2,1,0:T(8,128)(2,1)S(1)}, bf16[1,16,1536]{2,1,0:T(8,128)(2,1)S(1)}, u32[]{:S(2)}, u32[]{:S(2)}) %collective-permute-start.24) | collective-permute-done | bytes 49184 | tf_op jit(solution)/shard_map/ppermute | solution.py:662
  (112 shorter events, 50.2 us)
Async XLA Ops:
  4.6 6.1 %collective-permute-start = (bf16[1,16,1792]{2,1,0:T(8,128)(2,1)}, bf16[1,16,1792]{2,1,0:T(8,128)(2,1)S(1)}, u32[]{:S(2)}, u32[]{:S(2)}) collective-permute-start(bf16[1,16,1792]{2,1,0:T(8,128)(2,1)} %get-tuple-element.92), channel_id=1, source_target_pairs={{0,2},{1,5},{2,0},{3,7},{4,6},{5,1},{6,4},{7,3},{8,10},{9,13},{10,... | collective-permute-start | bytes 172040 | tf_op jit(solution)/shard_map/ppermute | solution.py:662
  11.5 5.8 %collective-permute-start.1 = (bf16[2,16,1792]{2,1,0:T(8,128)(2,1)S(1)}, bf16[2,16,1792]{2,1,0:T(8,128)(2,1)S(1)}, u32[]{:S(2)}, u32[]{:S(2)}) collective-permute-start(bf16[2,16,1792]{2,1,0:T(8,128)(2,1)S(1)} %pad_maximum_fusion.2), channel_id=1, source_target_pairs={{0,4},{1,3},{2,6},{3,1},{4,0},{5,7},{6,2},{7,5},{8,12},{9,11},{10,... | collective-permute-start | bytes 344072 | tf_op jit(solution)/shard_map/ppermute | solution.py:662
  17.3 7.0 %collective-permute-start.2 = (bf16[4,16,1792]{2,1,0:T(8,128)(2,1)S(1)}, bf16[4,16,1792]{2,1,0:T(8,128)(2,1)S(1)}, u32[]{:S(2)}, u32[]{:S(2)}) collective-permute-start(bf16[4,16,1792]{2,1,0:T(8,128)(2,1)S(1)} %get-tuple-element.197), channel_id=1, source_target_pairs={{0,8},{1,17},{2,10},{3,19},{4,12},{5,21},{6,14},{7,23},{8,0},{9,25... | collective-permute-start | bytes 688136 | tf_op jit(solution)/shard_map/ppermute | solution.py:662
  19.0 7.3 %collective-permute-start.5 = (bf16[1,16,5632]{2,1,0:T(8,128)(2,1)}, bf16[1,16,5632]{2,1,0:T(8,128)(2,1)S(1)}, u32[]{:S(2)}, u32[]{:S(2)}) collective-permute-start(bf16[1,16,5632]{2,1,0:T(8,128)(2,1)} %get-tuple-element.94), channel_id=1, source_target_pairs={{0,2},{1,5},{2,0},{3,7},{4,6},{5,1},{6,4},{7,3},{8,10},{9,13},{10,... | collective-permute-start | bytes 540680 | tf_op jit(solution)/shard_map/ppermute | solution.py:662
  24.3 8.5 %collective-permute-start.3 = (bf16[8,16,1792]{2,1,0:T(8,128)(2,1)S(1)}, bf16[8,16,1792]{2,1,0:T(8,128)(2,1)S(1)}, u32[]{:S(2)}, u32[]{:S(2)}) collective-permute-start(bf16[8,16,1792]{2,1,0:T(8,128)(2,1)S(1)} %get-tuple-element.191), channel_id=1, source_target_pairs={{0,16},{1,9},{2,18},{3,11},{4,20},{5,13},{6,22},{7,15},{8,24},{9,1... | collective-permute-start | bytes 1376264 | tf_op jit(solution)/shard_map/ppermute | solution.py:662
  27.3 12.3 %collective-permute-start.6 = (bf16[2,16,5632]{2,1,0:T(8,128)(2,1)S(1)}, bf16[2,16,5632]{2,1,0:T(8,128)(2,1)S(1)}, u32[]{:S(2)}, u32[]{:S(2)}) collective-permute-start(bf16[2,16,5632]{2,1,0:T(8,128)(2,1)S(1)} %pad_maximum_fusion.1), channel_id=1, source_target_pairs={{0,4},{1,3},{2,6},{3,1},{4,0},{5,7},{6,2},{7,5},{8,12},{9,11},{10,... | collective-permute-start | bytes 1081352 | tf_op jit(solution)/shard_map/ppermute | solution.py:662
  32.9 9.3 %collective-permute-start.4 = (bf16[16,16,1792]{2,1,0:T(8,128)(2,1)S(1)}, bf16[16,16,1792]{2,1,0:T(8,128)(2,1)S(1)}, u32[]{:S(2)}, u32[]{:S(2)}) collective-permute-start(bf16[16,16,1792]{2,1,0:T(8,128)(2,1)S(1)} %constant_dynamic-update-slice_fusion.7.refs_4_), channel_id=1, source_target_pairs={{0,1},{1,0},{2,3},{3,2},{4,5},{5,4},{6,7},{7,6},{8,9},{9,8},{10,11... | collective-permute-start | bytes 2752520 | tf_op jit(solution)/shard_map/ppermute | solution.py:662
  39.7 14.4 %collective-permute-start.7 = (bf16[4,16,5632]{2,1,0:T(8,128)(2,1)S(1)}, bf16[4,16,5632]{2,1,0:T(8,128)(2,1)S(1)}, u32[]{:S(2)}, u32[]{:S(2)}) collective-permute-start(bf16[4,16,5632]{2,1,0:T(8,128)(2,1)S(1)} %pad_maximum_fusion.refs_6_), channel_id=1, source_target_pairs={{0,8},{1,17},{2,10},{3,19},{4,12},{5,21},{6,14},{7,23},{8,0},{9,25... | collective-permute-start | bytes 2162696 | tf_op jit(solution)/shard_map/ppermute | solution.py:662
  55.0 19.0 %collective-permute-start.8 = (bf16[8,16,5632]{2,1,0:T(8,128)(2,1)S(1)}, bf16[8,16,5632]{2,1,0:T(8,128)(2,1)S(1)}, u32[]{:S(2)}, u32[]{:S(2)}) collective-permute-start(bf16[8,16,5632]{2,1,0:T(8,128)(2,1)S(1)} %get-tuple-element.179.refs_5_), channel_id=1, source_target_pairs={{0,16},{1,9},{2,18},{3,11},{4,20},{5,13},{6,22},{7,15},{8,24},{9,1... | collective-permute-start | bytes 4325384 | tf_op jit(solution)/shard_map/ppermute | solution.py:662
  75.3 8.0 %collective-permute-start.9 = (bf16[16,16,5632]{2,1,0:T(8,128)(2,1)}, bf16[16,16,5632]{2,1,0:T(8,128)(2,1)S(1)}, u32[]{:S(2)}, u32[]{:S(2)}) collective-permute-start(bf16[16,16,5632]{2,1,0:T(8,128)(2,1)} %constant_dynamic-update-slice_fusion.14.refs_5_), channel_id=1, source_target_pairs={{0,1},{1,0},{2,3},{3,2},{4,5},{5,4},{6,7},{7,6},{8,9},{9,8},{10,11... | collective-permute-start | bytes 8650760 | tf_op jit(solution)/shard_map/ppermute | solution.py:662
  114.8 20.8 %collective-permute-start.10 = (bf16[16,16,4096]{2,1,0:T(8,128)(2,1)}, bf16[16,16,4096]{2,1,0:T(8,128)(2,1)}, u32[]{:S(2)}, u32[]{:S(2)}) collective-permute-start(bf16[16,16,4096]{2,1,0:T(8,128)(2,1)} %get-tuple-element.124), channel_id=1, source_target_pairs={{0,1},{1,0},{2,3},{3,2},{4,5},{5,4},{6,7},{7,6},{8,9},{9,8},{10,11... | collective-permute-start | bytes 6291464 | tf_op jit(solution)/shard_map/ppermute | solution.py:662
  135.6 15.4 %collective-permute-start.12 = (bf16[16,16,1536]{2,1,0:T(8,128)(2,1)}, bf16[16,16,1536]{2,1,0:T(8,128)(2,1)S(1)}, u32[]{:S(2)}, u32[]{:S(2)}) collective-permute-start(bf16[16,16,1536]{2,1,0:T(8,128)(2,1)} %get-tuple-element.129), channel_id=1, source_target_pairs={{0,1},{1,0},{2,3},{3,2},{4,5},{5,4},{6,7},{7,6},{8,9},{9,8},{10,11... | collective-permute-start | bytes 2359304 | tf_op jit(solution)/shard_map/ppermute | solution.py:662
  138.9 14.8 %collective-permute-start.11 = (bf16[8,16,4096]{2,1,0:T(8,128)(2,1)S(1)}, bf16[8,16,4096]{2,1,0:T(8,128)(2,1)S(1)}, u32[]{:S(2)}, u32[]{:S(2)}) collective-permute-start(bf16[8,16,4096]{2,1,0:T(8,128)(2,1)S(1)} %get-tuple-element.165.refs_10_), channel_id=1, source_target_pairs={{0,16},{1,9},{2,18},{3,11},{4,20},{5,13},{6,22},{7,15},{8,24},{9,1... | collective-permute-start | bytes 3145736 | tf_op jit(solution)/shard_map/ppermute | solution.py:662
  152.1 13.4 %collective-permute-start.14 = (bf16[8,16,1536]{2,1,0:T(8,128)(2,1)}, bf16[8,16,1536]{2,1,0:T(8,128)(2,1)S(1)}, u32[]{:S(2)}, u32[]{:S(2)}) collective-permute-start(bf16[8,16,1536]{2,1,0:T(8,128)(2,1)} %get-tuple-element.171.refs_13_), channel_id=1, source_target_pairs={{0,16},{1,9},{2,18},{3,11},{4,20},{5,13},{6,22},{7,15},{8,24},{9,1... | collective-permute-start | bytes 1179656 | tf_op jit(solution)/shard_map/ppermute | solution.py:662
  154.8 12.7 %collective-permute-start.13 = (bf16[4,16,4096]{2,1,0:T(8,128)(2,1)S(1)}, bf16[4,16,4096]{2,1,0:T(8,128)(2,1)S(1)}, u32[]{:S(2)}, u32[]{:S(2)}) collective-permute-start(bf16[4,16,4096]{2,1,0:T(8,128)(2,1)S(1)} %get-tuple-element.167.refs_11_), channel_id=1, source_target_pairs={{0,8},{1,17},{2,10},{3,19},{4,12},{5,21},{6,14},{7,23},{8,0},{9,25... | collective-permute-start | bytes 1572872 | tf_op jit(solution)/shard_map/ppermute | solution.py:662
  166.2 14.8 %collective-permute-start.16 = (bf16[4,16,1536]{2,1,0:T(8,128)(2,1)S(1)}, bf16[4,16,1536]{2,1,0:T(8,128)(2,1)S(1)}, u32[]{:S(2)}, u32[]{:S(2)}) collective-permute-start(bf16[4,16,1536]{2,1,0:T(8,128)(2,1)S(1)} %get-tuple-element.177.refs_13_), channel_id=1, source_target_pairs={{0,8},{1,17},{2,10},{3,19},{4,12},{5,21},{6,14},{7,23},{8,0},{9,25... | collective-permute-start | bytes 589832 | tf_op jit(solution)/shard_map/ppermute | solution.py:662
  168.3 15.6 %collective-permute-start.15 = (bf16[2,16,4096]{2,1,0:T(8,128)(2,1)S(1)}, bf16[2,16,4096]{2,1,0:T(8,128)(2,1)S(1)}, u32[]{:S(2)}, u32[]{:S(2)}) collective-permute-start(bf16[2,16,4096]{2,1,0:T(8,128)(2,1)S(1)} %get-tuple-element.173.refs_11_), channel_id=1, source_target_pairs={{0,4},{1,3},{2,6},{3,1},{4,0},{5,7},{6,2},{7,5},{8,12},{9,11},{10,... | collective-permute-start | bytes 786440 | tf_op jit(solution)/shard_map/ppermute | solution.py:662
  181.7 12.1 %collective-permute-start.18 = (bf16[2,16,1536]{2,1,0:T(8,128)(2,1)S(1)}, bf16[2,16,1536]{2,1,0:T(8,128)(2,1)S(1)}, u32[]{:S(2)}, u32[]{:S(2)}) collective-permute-start(bf16[2,16,1536]{2,1,0:T(8,128)(2,1)S(1)} %get-tuple-element.187.refs_15_), channel_id=1, source_target_pairs={{0,4},{1,3},{2,6},{3,1},{4,0},{5,7},{6,2},{7,5},{8,12},{9,11},{10,... | collective-permute-start | bytes 294920 | tf_op jit(solution)/shard_map/ppermute | solution.py:662
  184.7 9.8 %collective-permute-start.17 = (bf16[1,16,4096]{2,1,0:T(8,128)(2,1)S(1)}, bf16[1,16,4096]{2,1,0:T(8,128)(2,1)S(1)}, u32[]{:S(2)}, u32[]{:S(2)}) collective-permute-start(bf16[1,16,4096]{2,1,0:T(8,128)(2,1)S(1)} %get-tuple-element.183.refs_13_), channel_id=1, source_target_pairs={{0,2},{1,5},{2,0},{3,7},{4,6},{5,1},{6,4},{7,3},{8,10},{9,13},{10,... | collective-permute-start | bytes 393224 | tf_op jit(solution)/shard_map/ppermute | solution.py:662
  199.3 9.1 %collective-permute-start.20 = (bf16[8,16,1792]{2,1,0:T(8,128)(2,1)S(1)}, bf16[8,16,1792]{2,1,0:T(8,128)(2,1)S(1)}, u32[]{:S(2)}, u32[]{:S(2)}) collective-permute-start(bf16[8,16,1792]{2,1,0:T(8,128)(2,1)S(1)} %get-tuple-element.169.refs_6_), channel_id=1, source_target_pairs={{0,16},{1,9},{2,18},{3,11},{4,20},{5,13},{6,22},{7,15},{8,24},{9,1... | collective-permute-start | bytes 1376264 | tf_op jit(solution)/shard_map/ppermute | solution.py:662
  208.6 6.1 %collective-permute-start.21 = (bf16[4,16,1792]{2,1,0:T(8,128)(2,1)S(1)}, bf16[4,16,1792]{2,1,0:T(8,128)(2,1)S(1)}, u32[]{:S(2)}, u32[]{:S(2)}) collective-permute-start(bf16[4,16,1792]{2,1,0:T(8,128)(2,1)S(1)} %get-tuple-element.176), channel_id=1, source_target_pairs={{0,8},{1,17},{2,10},{3,19},{4,12},{5,21},{6,14},{7,23},{8,0},{9,25... | collective-permute-start | bytes 688136 | tf_op jit(solution)/shard_map/ppermute | solution.py:662
  214.8 7.0 %collective-permute-start.22 = (bf16[2,16,1792]{2,1,0:T(8,128)(2,1)S(1)}, bf16[2,16,1792]{2,1,0:T(8,128)(2,1)S(1)}, u32[]{:S(2)}, u32[]{:S(2)}) collective-permute-start(bf16[2,16,1792]{2,1,0:T(8,128)(2,1)S(1)} %get-tuple-element.186), channel_id=1, source_target_pairs={{0,4},{1,3},{2,6},{3,1},{4,0},{5,7},{6,2},{7,5},{8,12},{9,11},{10,... | collective-permute-start | bytes 344072 | tf_op jit(solution)/shard_map/ppermute | solution.py:662
  222.4 8.5 %collective-permute-start.23 = (bf16[1,16,1792]{2,1,0:T(8,128)(2,1)S(1)}, bf16[1,16,1792]{2,1,0:T(8,128)(2,1)S(1)}, u32[]{:S(2)}, u32[]{:S(2)}) collective-permute-start(bf16[1,16,1792]{2,1,0:T(8,128)(2,1)S(1)} %get-tuple-element.189), channel_id=1, source_target_pairs={{0,2},{1,5},{2,0},{3,7},{4,6},{5,1},{6,4},{7,3},{8,10},{9,13},{10,... | collective-permute-start | bytes 172040 | tf_op jit(solution)/shard_map/ppermute | solution.py:662
  222.5 4.6 %collective-permute-start.24 = (bf16[1,16,1536]{2,1,0:T(8,128)(2,1)S(1)}, bf16[1,16,1536]{2,1,0:T(8,128)(2,1)S(1)}, u32[]{:S(2)}, u32[]{:S(2)}) collective-permute-start(bf16[1,16,1536]{2,1,0:T(8,128)(2,1)S(1)} %get-tuple-element.193), channel_id=1, source_target_pairs={{0,2},{1,5},{2,0},{3,7},{4,6},{5,1},{6,4},{7,3},{8,10},{9,13},{10,... | collective-permute-start | bytes 147464 | tf_op jit(solution)/shard_map/ppermute | solution.py:662
  (25 other events, 144.7 us)
